TPU v7x, 32 devices: a whole 2x2x4 slice. The times are simulated.
32 devices in a mesh: groups: 2 (over x), tensor: 16 (over z, y, core).
Axes of the slice: x: 2, y: 2, z: 4, core: 2. Of those that a mesh axis runs over, the one named last changes fastest.
Arguments:
- queries: bfloat16 [512, 16384], P('groups', 'tensor'), parts along dimension 0, may hold values from -7 to 7
- keys: bfloat16 [4096, 1024], P(('groups', 'tensor')), parts along dimension 0, may hold values from -6 to 6
- values: bfloat16 [4096, 1024], P(('groups', 'tensor')), parts along dimension 0, may hold values from -6 to 6
- lengths: int32 [32], P(('groups', 'tensor')), parts along dimension 0, may hold values from 64 to 128, as said below
- start_pos: int32 [2], P('groups'), parts along dimension 0, may hold values from 512 to 1792
- out_weight: bfloat16 [16384, 16384], P('tensor'), may hold values from -0.046875 to 0.046875
Outputs:
- layer_output: bfloat16 [512, 16384], P('groups'), parts along dimension 0
There are 2 independent parts, one for each index of `groups`. A program takes and returns all parts, laid end to end along the dimension named above; an argument that names none is the same for every part. Nothing has to cross between parts.
Inputs may be any that keep to these rules, and one draw needn't show every extreme that they name: `lengths`: each shard's prefix is at least half of its 128 slots; some shard is full and some holds exactly half.
All inputs are finite; a program needn't handle non-finite values.
Results may differ from a plain program's by a relative error of at most 0.014.
Values may be sent and summed in bfloat16 or wider, within the bound.
No kernel may reach another device: no remote copies, remote signals or barrier semaphores. Data moves between devices by JAX's collectives and lax.ppermute only.
A program may use at most 128 MiB of HBM per device.

v0:
```python
import jax
import jax.numpy as jnp
from jax import lax
from jax.sharding import PartitionSpec as P

HEADS = 128
KV_HEADS = 8
HEAD_DIM = 128


def shards(queries, keys, values, lengths, start_pos, out_weight):
    shard_slots = keys.shape[0]
    token_count = queries.shape[0]
    local_heads = queries.shape[1] // HEAD_DIM
    group_size = HEADS // KV_HEADS
    kv_head = lax.axis_index("tensor") * local_heads // group_size
    query_pos = start_pos[0] + lax.iota(jnp.int32, token_count)
    query_heads = queries.reshape(token_count, local_heads, HEAD_DIM)
    score_scale = HEAD_DIM ** (-0.5)
    key_all = lax.all_gather(keys, "tensor", axis=0, tiled=True)
    value_all = lax.all_gather(values, "tensor", axis=0, tiled=True)
    length_piece = lax.all_gather(lengths, "tensor", axis=0, tiled=True)
    key_rows = lax.dynamic_slice_in_dim(key_all, kv_head * HEAD_DIM, HEAD_DIM, 1)
    value_rows = lax.dynamic_slice_in_dim(value_all, kv_head * HEAD_DIM, HEAD_DIM, 1)
    row_total = key_rows.shape[0]
    live_slot = (lax.iota(jnp.int32, shard_slots)[None, :] < length_piece[:, None]).reshape(
        row_total
    )
    positions = lax.iota(jnp.int32, row_total)
    allowed = live_slot[None, :] & (positions[None, :] <= query_pos[:, None])
    allowed = allowed[:, None, :]
    scores = (
        jnp.einsum("thd,rd->thr", query_heads, key_rows, preferred_element_type=jnp.float32)
        * score_scale
    )
    scores = jnp.where(allowed, scores, -1e30)
    top_old = jnp.full((token_count, local_heads), -1e30, jnp.float32)
    top_new = jnp.maximum(top_old, jnp.max(scores, axis=-1))
    raw_weights = jnp.where(allowed, jnp.exp(scores - top_new[..., None]), 0.0)
    total_new = jnp.sum(raw_weights, axis=-1)
    mixed = jnp.einsum(
        "thr,rd->thd",
        raw_weights.astype(jnp.bfloat16),
        value_rows,
        preferred_element_type=jnp.float32,
    )
    final_state = (top_new, total_new, mixed)
    _, row_sums, accumulated = final_state
    attended = (
        (accumulated / row_sums[..., None])
        .astype(jnp.bfloat16)
        .reshape(token_count, local_heads * HEAD_DIM)
    )
    partial_value = jnp.dot(attended, out_weight, preferred_element_type=jnp.float32).astype(
        jnp.bfloat16
    )
    widened = lax.optimization_barrier(partial_value).astype(jnp.float32)
    summed = lax.psum_scatter(
        widened.astype(jnp.bfloat16), "tensor", scatter_dimension=0, tiled=True
    )
    return lax.all_gather(summed, "tensor", axis=0, tiled=True)


def solution(mesh):
    in_specs = (
        P("groups", "tensor"),
        P(("groups", "tensor"), None),
        P(("groups", "tensor"), None),
        P(("groups", "tensor")),
        P("groups"),
        P("tensor", None),
    )
    out_specs = P("groups", None)
    return jax.shard_map(shards, mesh=mesh, in_specs=in_specs, out_specs=out_specs, check_vma=False)
```

profile of v0, /device:TPU:1, one launch (start us, length us, event | category | flops | bytes accessed | tf_op | source)
XLA Modules:
  0.0 343.2 jit_solution(5949434899442698958)
XLA Ops:
  6.5 0.7 all-gather.4.cloned.1.call-update
  7.3 0.0 all-gather.6.cloned.1.call-start
  7.3 1.8 copy.8
  9.1 0.0 all-gather.6.cloned.1.call-update
  9.1 0.0 reduce-scatter.2.cloned.1.call-start
  9.8 1.3 dynamic-slice
  11.1 0.8 dynamic-update-slice
  11.9 10.8 %all-reduce = s32[16]{0:T(128)S(1)} all-reduce(s32[16]{0:T(128)S(1)} %dynamic-update-slice), channel_id=1, replica_groups=mesh['groups'=2,'tensor'=16] {'tensor'}, use_global_device_ids=true, to_apply=%add | all-reduce | flops 16 | bytes 128
  23.4 0.1 fusion.16
  23.5 0.5 fusion.6
  23.9 38.7 %all-gather.4.cloned.1.call-done = bf16[2048,1024]{1,0:T(8,128)(2,1)} async-done(((bf16[128,1024]{1,0:T(8,128)(2,1)}), bf16[2048,1024]{1,0:T(8,128)(2,1)}) %all-gather.4.cloned.1.call-update) | async-done | bytes 4194320 | tf_op jit(solution)/shard_map/all_gather | solution.py:20
  62.6 3.7 %fusion = (f32[256,8]{0,1:T(8,128)S(1)}, f32[2048,256,8]{1,0,2:T(8,128)S(1)}) fusion(pred[256,2048]{0,1:T(8,128)(4,1)S(1)} %fusion.6, bf16[2048,1024]{1,0:T(8,128)(2,1)} %all-gather.4.cloned.1.call-done, s32[]{:T(128)S(6)} %select_n.17, bf16[256,1024]{1,0:T(8,128)(2,1)S(1)} %copy-done), kind=kOutput, calls=%fused_computation.3 | convolution fusion | flops 1086322688 | bytes 18358276 | tf_op jit(solution)/shard_map/thd,rd->thr/dot_general | solution.py:33
  66.3 5.8 %copy-done.2 = f32[2048,256,8]{1,0,2:T(8,128)} copy-done((f32[2048,256,8]{1,0,2:T(8,128)}, f32[2048,256,8]{1,0,2:T(8,128)S(1)}, u32[]{:S(2)}) %copy-start.2) | copy-done | bytes 16777240
  72.1 4.0 %fusion.1 = f32[256,8]{0,1:T(8,128)S(1)} fusion(f32[2048,256,8]{1,0,2:T(8,128)S(1)} %get-tuple-element.6, f32[256,8]{0,1:T(8,128)S(1)} %broadcast_maximum_fusion, pred[256,2048]{0,1:T(8,128)(4,1)S(1)} %fusion.6), kind=kLoop, calls=%fused_computation.4 | loop fusion | flops 20969472 | bytes 17317888 | tf_op jit(solution)/shard_map/reduce_sum | solution.py:40
  76.1 40.4 %all-gather.6.cloned.1.call-done = bf16[2048,1024]{0,1:T(8,128)(2,1)} async-done(((bf16[128,1024]{0,1:T(8,128)(2,1)}), bf16[2048,1024]{0,1:T(8,128)(2,1)}) %all-gather.6.cloned.1.call-update) | async-done | bytes 4194320 | tf_op jit(solution)/shard_map/all_gather | solution.py:21
  116.5 10.3 %divide_convert_fusion = bf16[256,8,128]{0,2,1:T(8,128)(2,1)S(1)} fusion(f32[2048,256,8]{1,0,2:T(8,128)} %copy-done.2, f32[256,8]{0,1:T(8,128)S(1)} %broadcast_maximum_fusion, pred[256,2048]{0,1:T(8,128)(4,1)S(1)} %fusion.6, f32[256,8]{0,1:T(8,128)S(1)} %fusion.1, bf16[2048,1024]{0,1:T(8,128)(2,1)} %all-gather.6.cloned.1.call-done, s32[]{:T(128)S(6)} %select_n.17), kind=kOutput, calls=%fused_computation.10 | convolution fusion | flops 1095237632 | bytes 18366468 | tf_op jit(solution)/shard_map/thr,rd->thd/dot_general | solution.py:41
  126.8 0.0 copy-start.1
  126.8 22.4 %convolution_convert_fusion = bf16[256,16384]{1,0:T(8,128)(2,1)} fusion(bf16[256,1024]{0,1:T(8,128)(2,1)S(1)} %bitcast.38, bf16[1024,16384]{1,0:T(8,128)(2,1)} %param.11), kind=kOutput, calls=%fused_computation | convolution fusion | flops 8594128896 | bytes 42467328 | tf_op jit(solution)/shard_map/dot_general | solution.py:54
  149.3 0.0 reduce-scatter.2.cloned.1.call-update
  149.3 0.0 all-gather.8.cloned.1.call-start
  149.4 102.6 %reduce-scatter.2.cloned.1.call-done = bf16[16,16384]{1,0:T(8,128)(2,1)} async-done(((bf16[256,16384]{1,0:T(8,128)(2,1)}), bf16[16,16384]{1,0:T(8,128)(2,1)}) %reduce-scatter.2.cloned.1.call-update) | async-done | bytes 524304 | tf_op jit(solution)/shard_map/reduce_scatter | solution.py:58
  251.9 0.0 all-gather.8.cloned.1.call-update
  252.0 77.0 %all-gather.8.cloned.1.call-done = bf16[256,16384]{1,0:T(8,128)(2,1)} async-done(((bf16[16,16384]{1,0:T(8,128)(2,1)}), bf16[256,16384]{1,0:T(8,128)(2,1)}) %all-gather.8.cloned.1.call-update) | async-done | bytes 8388624 | tf_op jit(solution)/shard_map/all_gather | solution.py:61
  329.0 7.7 %copy.22 = bf16[256,16384]{1,0:T(8,128)(2,1)} copy(bf16[256,16384]{1,0:T(8,128)(2,1)} %all-gather.8.cloned.1.call-done) | data formatting | bytes 16777216
  (8 shorter events, 0.0 us)
Async XLA Ops:
  6.5 56.1 %copy-start = (bf16[256,1024]{1,0:T(8,128)(2,1)S(1)}, bf16[256,1024]{1,0:T(8,128)(2,1)}, u32[]{:S(2)}) copy-start(bf16[256,1024]{1,0:T(8,128)(2,1)} %param.6) | copy-start | bytes 1572868
  6.5 56.1 %all-gather.4.cloned.1.call-start = ((), (), s32[]{:S(2)}) async-start(), calls=%async_computation.1 | async-start | bytes 4456448 | tf_op jit(solution)/shard_map/all_gather | solution.py:20
  7.3 109.2 %all-gather.6.cloned.1.call-start = ((), (), s32[]{:S(2)}) async-start(), calls=%async_computation.2 | async-start | bytes 4456448 | tf_op jit(solution)/shard_map/all_gather | solution.py:21
  9.1 242.8 %reduce-scatter.2.cloned.1.call-start = ((), (), s32[]{:S(2)}) async-start(), calls=%async_computation.3 | async-start | bytes 8912896 | tf_op jit(solution)/shard_map/reduce_scatter | solution.py:58
  66.3 5.8 %copy-start.2 = (f32[2048,256,8]{1,0,2:T(8,128)}, f32[2048,256,8]{1,0,2:T(8,128)S(1)}, u32[]{:S(2)}) copy-start(f32[2048,256,8]{1,0,2:T(8,128)S(1)} %get-tuple-element.6) | copy-start | bytes 50331652
  126.8 209.8 %copy-start.1 = (bf16[256,1024]{1,0:T(8,128)(2,1)S(1)}, bf16[256,1024]{1,0:T(8,128)(2,1)}, u32[]{:S(2)}) copy-start(bf16[256,1024]{1,0:T(8,128)(2,1)} %param.6) | copy-start | bytes 1572868
  149.3 179.7 %all-gather.8.cloned.1.call-start = ((), (), s32[]{:S(2)}) async-start(), calls=%async_computation.4 | async-start | bytes 8912896 | tf_op jit(solution)/shard_map/all_gather | solution.py:61
Sparse Core Ops, SparseCore 0:
  9.5 53.0 all-gather.3
  64.8 51.7 all-gather.5
  149.4 102.4 reduce-scatter.1
  254.0 75.0 all-gather.7
where the time goes:
time: 344 us; the launch traced here: 343 us
  waiting for transfers between devices  259 us (75%)
  matrix products  36.4 us (11%)
  local copies, waits for them, and re-layouts  17.4 us (5%)
  between operations  14.5 us (4%)
  blocking collectives  10.8 us (3%)
  other arithmetic  4.55 us (1%)
    reduce_scatter x1, waiting for transfers between devices, shards(): lax.psum_scatter(widened.astype(jnp.bfloat16), 'tensor', scatter_dimensio...  103 us
    all_gather x1, waiting for transfers between devices, shards(): return lax.all_gather(summed, 'tensor', axis=0, tiled=True)  77 us
    all_gather x1, waiting for transfers between devices, shards(): value_all = lax.all_gather(values, 'tensor', axis=0, tiled=True)  40.4 us
    all_gather x1, waiting for transfers between devices, shards(): key_all = lax.all_gather(keys, 'tensor', axis=0, tiled=True)  38.7 us
    dot_general x1, matrix products, shards(): jnp.dot(attended, out_weight, preferred_element_type=jnp.float32)  22.4 us
    unnamed x11, local copies, waits for them, and re-layouts  17.4 us
    unnamed x1, blocking collectives  10.8 us
    dot_general x1, matrix products, shards(): jnp.einsum('thr,rd->thd', raw_weights.astype(jnp.bfloat16), value_rows, p...  10.3 us
  transfers between devices with their start and end apart: 4, of which 4 were waited for; matrix products, arithmetic and copies ran while one was open for 4% of the time, Pallas kernels for 0%

commit v1 on v0

v1 whole, which is shorter than its diff:
```python
import functools
import math

import jax
import jax.numpy as jnp
from jax import lax
from jax.experimental import pallas as pl
from jax.experimental.pallas import tpu as pltpu
from jax.sharding import PartitionSpec as P

HEADS = 128
KV_HEADS = 8
HEAD_DIM = 128
GROUP = HEADS // KV_HEADS
FLAG_ROWS = 16
CHUNKS = 8
BLOCK_COLS = 512
SLOTS = 8
VMEM_LIMIT = 32 * 1024 * 1024


def pack_kernel(heads_ref, lengths_ref, k_ref, v_ref, *out_refs):
    slots = k_ref.shape[0]
    length = jnp.full((FLAG_ROWS, HEAD_DIM), lengths_ref[0], jnp.int32)
    length = length.astype(jnp.float32).astype(jnp.bfloat16)
    for m, out in enumerate(out_refs):
        cols = pl.ds(pl.multiple_of(heads_ref[m] * HEAD_DIM, HEAD_DIM), HEAD_DIM)
        out[:slots, :] = k_ref[:, cols]
        out[slots : 2 * slots, :] = v_ref[:, cols]
        out[2 * slots :, :] = length


def pack(heads, lengths, keys, values):
    slots = keys.shape[0]
    piece = jax.ShapeDtypeStruct((2 * slots + FLAG_ROWS, HEAD_DIM), jnp.bfloat16)
    smem = pl.BlockSpec(memory_space=pltpu.SMEM)
    vmem = pl.BlockSpec(memory_space=pltpu.VMEM)
    return pl.pallas_call(
        pack_kernel,
        out_shape=[piece] * heads.shape[0],
        in_specs=[smem, smem, vmem, vmem],
        out_specs=[vmem] * heads.shape[0],
        compiler_params=pltpu.CompilerParams(vmem_limit_bytes=VMEM_LIMIT),
        name="pack_kv",
    )(heads, lengths, keys, values)


def attention_kernel(count, scalars_ref, q_ref, *refs):
    pieces, (out_ref, keys, values, bias) = refs[:count], refs[count:]
    tokens = q_ref.shape[0]
    half = tokens // 2
    slots = (pieces[0].shape[0] - FLAG_ROWS) // 2
    start, core = scalars_ref[0], scalars_ref[1]
    token = lax.broadcasted_iota(jnp.int32, (tokens, slots), 0) + start
    lane = lax.broadcasted_iota(jnp.int32, (tokens, slots), 1)
    lane_row = lax.broadcasted_iota(jnp.int32, (1, slots), 1).astype(jnp.float32)
    for i, piece in enumerate(pieces):
        rows = slice(i * slots, (i + 1) * slots)
        keys[rows, :] = piece[:slots, :]
        values[rows, :] = piece[slots : 2 * slots, :]
        length = piece[2 * slots :, :].astype(jnp.float32)[:1, :slots]
        dead = jnp.where(lane_row < length, 0.0, -1e30)
        seen = lane + scalars_ref[2 + i] * slots <= token
        bias[:, rows] = jnp.where(seen, dead, -1e30)
    factor = HEAD_DIM ** (-0.5) * math.log2(math.e)
    for head in range(q_ref.shape[1] // HEAD_DIM):
        cols = slice(head * HEAD_DIM, (head + 1) * HEAD_DIM)
        for block in range(2):
            rows = slice(block * half, (block + 1) * half)
            scores = lax.dot_general(
                q_ref[rows, cols],
                keys[...],
                (((1,), (1,)), ((), ())),
                preferred_element_type=jnp.float32,
            )
            scores = scores + bias[rows, :]
            top = jnp.max(scores, axis=-1, keepdims=True)
            weights = jnp.exp2((scores - top) * factor)
            total = jnp.sum(weights, axis=-1, keepdims=True)
            mixed = jnp.dot(
                weights.astype(jnp.bfloat16), values[...], preferred_element_type=jnp.float32
            )
            place = pl.ds(pl.multiple_of((core ^ block) * half, half), half)
            out_ref[place, cols] = (mixed / total).astype(jnp.bfloat16)


def attention(scalars, queries, pieces):
    tokens, width = queries.shape
    slots = (pieces[0].shape[0] - FLAG_ROWS) // 2
    count = len(pieces)
    smem = pl.BlockSpec(memory_space=pltpu.SMEM)
    vmem = pl.BlockSpec(memory_space=pltpu.VMEM)
    return pl.pallas_call(
        functools.partial(attention_kernel, count),
        out_shape=jax.ShapeDtypeStruct((tokens, width), jnp.bfloat16),
        in_specs=[smem] + [vmem] * (1 + count),
        out_specs=vmem,
        scratch_shapes=[
            pltpu.VMEM((count * slots, HEAD_DIM), jnp.bfloat16),
            pltpu.VMEM((count * slots, HEAD_DIM), jnp.bfloat16),
            pltpu.VMEM((tokens, count * slots), jnp.float32),
        ],
        compiler_params=pltpu.CompilerParams(vmem_limit_bytes=VMEM_LIMIT),
        cost_estimate=pl.CostEstimate(
            flops=4 * tokens * width * count * slots,
            bytes_accessed=4 * tokens * width + 4 * count * slots * HEAD_DIM,
            transcendentals=tokens * count * slots * (width // HEAD_DIM),
        ),
        name="attention",
    )(scalars, queries, *pieces)


def in_order(kernel, ins, outs):
    def body(*refs):
        inputs, rest = refs[:ins], refs[ins + 1 :]
        kernel(*inputs, *rest[:outs], *rest[outs + 1 :])
        rest[outs][...] = jnp.zeros_like(rest[outs])

    return body


def call(kernel, turn, args, in_specs, out_shapes, out_specs, name, scratch=(), aliases=None):
    turn_shape = jax.ShapeDtypeStruct((8, 128), jnp.float32)
    *results, turn = pl.pallas_call(
        in_order(kernel, len(args), len(out_shapes)),
        out_shape=[*out_shapes, turn_shape],
        in_specs=[*in_specs, pl.BlockSpec(memory_space=pl.ANY)],
        out_specs=[*out_specs, VMEM],
        scratch_shapes=list(scratch),
        input_output_aliases=aliases or {},
        compiler_params=pltpu.CompilerParams(vmem_limit_bytes=VMEM_LIMIT),
        cost_estimate=pl.CostEstimate(flops=0, bytes_accessed=1 << 17, transcendentals=0),
        name=name,
    )(*args, turn)
    return results, turn


VMEM = pl.BlockSpec(memory_space=pltpu.VMEM)
SMEM = pl.BlockSpec(memory_space=pltpu.SMEM)
ANY = pl.BlockSpec(memory_space=pl.ANY)


def project_kernel(bases, width, where_ref, a_ref, w_ref, *refs):
    outs, (buffer, sems) = refs[:-2], refs[-2:]
    half = a_ref.shape[0] // 2
    side = where_ref[1]
    tile = min(width, BLOCK_COLS)
    blocks = [
        (number, part, i)
        for number in range(len(bases))
        for part in range(2)
        for i in range(width // tile)
    ]
    copies = []
    for at, (number, part, i) in enumerate(blocks):
        first = bases[number] + (side ^ (1 - part)) * width + i * tile
        cols = pl.ds(pl.multiple_of(first, tile), tile)
        slot = at % buffer.shape[0]
        copies.append(pltpu.make_async_copy(w_ref.at[:, cols], buffer.at[slot], sems.at[slot]))
    for copy in copies[: buffer.shape[0]]:
        copy.start()
    for at, (number, part, i) in enumerate(blocks):
        copies[at].wait()
        product = jnp.dot(
            a_ref[...], buffer[at % buffer.shape[0]], preferred_element_type=jnp.float32
        ).astype(jnp.bfloat16)
        if at + buffer.shape[0] < len(blocks):
            copies[at + buffer.shape[0]].start()
        cols = slice(i * tile, (i + 1) * tile)
        outs[2 * number][part, :, cols] = product[:half]
        outs[2 * number + 1][part, :, cols] = product[half:]


def project(turn, where, attended, weight, bases, width):
    tokens, depth = attended.shape
    out = jax.ShapeDtypeStruct((2, tokens // 2, width), jnp.bfloat16)
    count = 2 * len(bases)
    tile = min(width, BLOCK_COLS)
    slots = min(SLOTS, count * width // tile)
    return call(
        functools.partial(project_kernel, bases, width),
        turn,
        [where, attended, weight],
        [SMEM, VMEM, ANY],
        [out] * count,
        [VMEM] * count,
        "project",
        [pltpu.VMEM((slots, depth, tile), jnp.bfloat16), pltpu.SemaphoreType.DMA((slots,))],
    )


def plus(*terms):
    total = terms[0].astype(jnp.float32)
    for term in terms[1:]:
        total = total + term.astype(jnp.float32)
    return total.astype(jnp.bfloat16)


def leave(where, own, core, out):
    out[...] = plus(own[0], core[0])


def join(where, own, core, beside, out):
    out[...] = plus(own[1], core[1], beside[...])


def inward(where, own, core, beside, near, out):
    out[...] = plus(own[1], core[1], beside[...], near[...])


def middle(where, own, across, out):
    out[...] = plus(own[...], across[...])


def join_and_middle(where, own, core, beside, near, across, out):
    inner = where[2]

    @pl.when(inner == 0)
    def _():
        join(where, own, core, beside, out)

    @pl.when(inner == 1)
    def _():
        middle(where, near, across, out)


def choose(where, near, own, out):
    inner = where[2]

    @pl.when(inner == 0)
    def _():
        out[...] = near[...]

    @pl.when(inner == 1)
    def _():
        out[...] = own[...]


def stack(where, own, beside, out):
    out[0] = own[...]
    out[1] = beside[...]


def tick_kernel(jobs, where_ref, *refs):
    at = sum(len(ins) for _, ins, _ in jobs)
    outs = refs[at:]
    at = 0
    for (job, ins, _), out in zip(jobs, outs):
        job(where_ref, *refs[at : at + len(ins)], out)
        at += len(ins)


def tick(turn, where, jobs):
    arrays = [x for _, ins, _ in jobs for x in ins]
    outs = [jax.ShapeDtypeStruct(shape, jnp.bfloat16) for _, _, shape in jobs]
    return call(
        functools.partial(tick_kernel, jobs),
        turn,
        [where, *arrays],
        [SMEM] + [VMEM] * len(arrays),
        outs,
        [VMEM] * len(outs),
        "tick",
    )


def place_kernel(base, width, where_ref, mine, theirs, *refs):
    out_ref, sems = refs[-2:]
    half = mine.shape[1]
    core, side = where_ref[0], where_ref[1]
    copies = []
    for i in range(4):
        row = pl.multiple_of((core ^ (i // 2)) * half, half)
        col = pl.multiple_of(base + (side ^ (i % 2)) * width, width)
        source = (mine, theirs)[i // 2].at[i % 2]
        copies.append(
            pltpu.make_async_copy(
                source, out_ref.at[pl.ds(row, half), pl.ds(col, width)], sems.at[i]
            )
        )
    for copy in copies:
        copy.start()
    for copy in copies:
        copy.wait()


def place(turn, where, mine, theirs, out, base, shape):
    width = mine.shape[2]
    given = [] if out is None else [out]
    (out,), turn = call(
        functools.partial(place_kernel, base, width),
        turn,
        [where, mine, theirs, *given],
        [SMEM, ANY, ANY] + [ANY] * len(given),
        [jax.ShapeDtypeStruct(shape, jnp.bfloat16)],
        [ANY],
        "place",
        [pltpu.SemaphoreType.DMA((4,))],
        {3: 0} if given else None,
    )
    return out, turn


def shards(devices, queries, keys, values, lengths, start_pos, out_weight):
    slots = keys.shape[0]
    tokens = queries.shape[0]
    columns = out_weight.shape[1]
    local_heads = queries.shape[1] // HEAD_DIM
    chips = devices // 2
    line = chips // 2
    me = lax.axis_index("tensor")
    core, chip = me % 2, me // 2
    side, spot = chip % 2, chip // 2

    def swap(x, bits):
        return lax.ppermute(x, "tensor", [(d, d ^ bits) for d in range(devices)])

    def along(x, pairs):
        perm = [(a * 4 + i, b * 4 + i) for a, b in pairs for i in range(4)]
        return lax.ppermute(x, "tensor", perm)

    others = chip ^ jnp.arange(chips, dtype=jnp.int32)
    heads = others * (2 * local_heads) // GROUP
    packed = pack(heads, lengths, keys, values)
    order = sorted(range(1, chips), reverse=True)
    direct = {0: packed[0]}
    for m in order:
        direct[m] = swap(packed[m], 2 * m)
    pieces, shard_ids = [], []
    for m in [0] + order:
        pieces += [direct[m], swap(direct[m], 1)]
        shard_ids += [2 * others[m] + core, 2 * others[m] + (core ^ 1)]
    scalars = jnp.stack([start_pos[0], core, *shard_ids]).astype(jnp.int32)
    attended = attention(scalars, queries, pieces)

    if line != 4:
        partial_value = jnp.dot(attended, out_weight, preferred_element_type=jnp.float32)
        partial_value = jnp.roll(partial_value.astype(jnp.bfloat16), core * (tokens // 2), axis=0)
        summed = lax.psum_scatter(partial_value, "tensor", scatter_dimension=0, tiled=True)
        return lax.all_gather(summed, "tensor", axis=0, tiled=True)

    width = columns // (2 * CHUNKS)
    inner = (spot == 1) | (spot == 2)
    where = jnp.stack([core, side, inner.astype(jnp.int32)]).astype(jnp.int32)
    shape = (tokens // 2, width)
    chunks = [{"base": 2 * chunk * width} for chunk in range(CHUNKS)]
    turn = jnp.zeros((8, 128), jnp.float32)
    out = None

    def project_some(turn, some):
        results, turn = project(
            turn, where, attended, out_weight, [c["base"] for c in some], width
        )
        for i, c in enumerate(some):
            c["own"] = results[2 * i]
            c["core"] = swap(results[2 * i + 1], 1)
        return turn

    def step(turn, time, lane):
        at = {time - i: c for i, c in enumerate(lane)}
        jobs, after = [], []
        if 0 in at:
            c = at[0]
            jobs.append((leave, [c["own"], c["core"]], shape))
            after.append((c, "beside", lambda x: swap(x, 2)))
        if 2 in at:
            c = at[2]
            jobs.append((inward, [c["own"], c["core"], c["beside"], c["near"]], shape))
            after.append((c, "across", lambda x: along(x, [(1, 2), (2, 1)])))
        early, late = at.get(1), at.get(3)
        if early or late:
            ins = [early["own"], early["core"], early["beside"]] if early else []
            ins += [late["across_sent"], late["across"]] if late else []
            job = join_and_middle if early and late else join if early else middle
            jobs.append((job, ins, shape))
            after.append(((early, late), "near", lambda x: swap(x, 4)))
        if 4 in at:
            c = at[4]
            jobs.append((choose, [c["near"], c["near_sent"]], shape))
            after.append((c, "beside", lambda x: swap(x, 2)))
        if 5 in at:
            c = at[5]
            jobs.append((stack, [c["beside_sent"], c["beside"]], (2, *shape)))
            after.append((c, "theirs", lambda x: swap(x, 1)))
        if not jobs:
            return turn
        results, turn = tick(turn, where, jobs)
        for (owner, key, send), x in zip(after, results):
            got = send(x)
            for c in owner if isinstance(owner, tuple) else (owner,):
                if c is not None:
                    c[key], c[key + "_sent"] = got, x
        return turn

    lanes = [chunks[0::2], chunks[1::2]]
    turn = project_some(turn, chunks[:2])
    for time in range(len(lanes[0]) + 6):
        for lane in lanes:
            turn = step(turn, time, lane)
            if 0 <= time - 6 < len(lane):
                c = lane[time - 6]
                out, turn = place(
                    turn, where, c["theirs_sent"], c["theirs"], out, c["base"], (tokens, columns)
                )
        if time == 0:
            turn = project_some(turn, chunks[2:])
    return out


def solution(mesh):
    in_specs = (
        P("groups", "tensor"),
        P(("groups", "tensor"), None),
        P(("groups", "tensor"), None),
        P(("groups", "tensor")),
        P("groups"),
        P("tensor", None),
    )
    out_specs = P("groups", None)
    return jax.shard_map(
        functools.partial(shards, mesh.shape["tensor"]),
        mesh=mesh,
        in_specs=in_specs,
        out_specs=out_specs,
        check_vma=False,
    )
```

time: 344 us -> 180 us (0.52)
  waiting for transfers between devices: 259 us -> 21.8 us
  starting transfers between devices: 0.12 us -> 93.4 us
  Pallas kernels: 0 us -> 53.1 us
  matrix products: 36.4 us -> 0 us
  local copies, waits for them, and re-layouts: 17.4 us -> 3.71 us
  blocking collectives: 10.8 us -> 0 us
  between operations: 14.5 us -> 7.13 us
  other arithmetic: 4.55 us -> 0.09 us
    all_gather x3 -> x0, waiting for transfers between devices: 156 us -> none  [the longest x1 77 us: shards(): return lax.all_gather(summed, 'tensor', axis=0, tiled=True)]
    reduce_scatter x1 -> x0, waiting for transfers between devices: 103 us -> none  [shards(): lax.psum_scatter(widened.astype(jnp.bfloat16), 'tensor', scatter_dimensio...]
    ppermute x0 -> x67, starting transfers between devices: none -> 93.4 us  [the longest x59 88.1 us: swap(): return lax.ppermute(x, 'tensor', [(d, d ^ bits) for d in range(devices)])]
    pallas_call x0 -> x30, Pallas kernels: none -> 53.1 us  [the longest x28 43.6 us: call(): pl.pallas_call(in_order(kernel, len(args), len(out_shapes)), out_shape=[*...]
    dot_general x3 -> x0, matrix products: 36.4 us -> none  [the longest x1 22.4 us: shards(): jnp.dot(attended, out_weight, preferred_element_type=jnp.float32)]
    ppermute x0 -> x67, waiting for transfers between devices: none -> 21.8 us  [the longest x59 21.8 us: swap(): return lax.ppermute(x, 'tensor', [(d, d ^ bits) for d in range(devices)])]
    unnamed x11 -> x6, local copies, waits for them, and re-layouts: 17.4 us -> 2.94 us
    unnamed x1 -> x0, blocking collectives: 10.8 us -> none
  transfers between devices with their start and end apart: 4 -> 67, of which waited for: 4 -> 18; matrix products, arithmetic and copies ran while one was open for 4% -> 0% of each run, Pallas kernels for 0% -> 13%
where the time goes in v1:
time: 180 us; the launch traced here: 179 us
  starting transfers between devices  93.4 us (52%)
  Pallas kernels  53.1 us (30%)
  waiting for transfers between devices  21.8 us (12%)
  between operations  7.13 us (4%)
  local copies, waits for them, and re-layouts  3.71 us (2%)
    ppermute x59, starting transfers between devices, swap(): return lax.ppermute(x, 'tensor', [(d, d ^ bits) for d in range(devices)])  88.1 us
    pallas_call x28, Pallas kernels, call(): pl.pallas_call(in_order(kernel, len(args), len(out_shapes)), out_shape=[*...  43.6 us
    ppermute x59, waiting for transfers between devices, swap(): return lax.ppermute(x, 'tensor', [(d, d ^ bits) for d in range(devices)])  21.8 us
    pallas_call x1, Pallas kernels, attention(): pl.pallas_call(functools.partial(attention_kernel, count), out_shape=jax....  8.87 us
    ppermute x8, starting transfers between devices, along(): return lax.ppermute(x, 'tensor', perm)  5.35 us
  transfers between devices with their start and end apart: 67, of which 18 were waited for; matrix products, arithmetic and copies ran while one was open for 0% of the time, Pallas kernels for 13%

profile of v1, /device:TPU:1, one launch (start us, length us, event | category | flops | bytes accessed | tf_op | source)
XLA Modules:
  0.0 179.3 jit_solution(745285129796947952)
XLA Ops:
  3.3 3.1 %collective-permute-start.9 = (bf16[272,128]{1,0:T(8,128)(2,1)S(1)}, bf16[272,128]{1,0:T(8,128)(2,1)S(1)}, u32[]{:S(2)}, u32[]{:S(2)}) collective-permute-start(bf16[272,128]{1,0:T(8,128)(2,1)S(1)} %get-tuple-element.113), channel_id=1, source_target_pairs={{0,6},{1,7},{2,4},{3,5},{4,2},{5,3},{6,0},{7,1},{8,14},{9,15},{10,... | collective-permute-start | bytes 208904 | tf_op jit(solution)/shard_map/ppermute | solution.py:316
  6.8 4.3 %collective-permute-start.1 = (bf16[272,128]{1,0:T(8,128)(2,1)S(1)}, bf16[272,128]{1,0:T(8,128)(2,1)S(1)}, u32[]{:S(2)}, u32[]{:S(2)}) collective-permute-start(bf16[272,128]{1,0:T(8,128)(2,1)S(1)} %get-tuple-element.109), channel_id=1, source_target_pairs={{0,14},{1,15},{2,12},{3,13},{4,10},{5,11},{6,8},{7,9},{8,6},{9,7},... | collective-permute-start | bytes 208904 | tf_op jit(solution)/shard_map/ppermute | solution.py:316
  13.5 2.4 %collective-permute-start = (bf16[272,128]{1,0:T(8,128)(2,1)S(1)}, bf16[272,128]{1,0:T(8,128)(2,1)S(1)}, u32[]{:S(2)}, u32[]{:S(2)}) collective-permute-start(bf16[272,128]{1,0:T(8,128)(2,1)S(1)} %get-tuple-element.108.refs_0_), channel_id=1, source_target_pairs={{0,1},{1,0},{2,3},{3,2},{4,5},{5,4},{6,7},{7,6},{8,9},{9,8},{10,11... | collective-permute-start | bytes 208904 | tf_op jit(solution)/shard_map/ppermute | solution.py:316
  16.1 3.6 %collective-permute-start.12 = (bf16[272,128]{1,0:T(8,128)(2,1)S(1)}, bf16[272,128]{1,0:T(8,128)(2,1)S(1)}, u32[]{:S(2)}, u32[]{:S(2)}) collective-permute-start(bf16[272,128]{1,0:T(8,128)(2,1)S(1)} %collective-permute-done.11.refs_12_), channel_id=1, source_target_pairs={{0,1},{1,0},{2,3},{3,2},{4,5},{5,4},{6,7},{7,6},{8,9},{9,8},{10,11... | collective-permute-start | bytes 208904 | tf_op jit(solution)/shard_map/ppermute | solution.py:316
  29.8 8.9 %attention.1.refs_1_ = bf16[256,1024]{1,0:T(8,128)(2,1)S(1)} custom-call(s32[18]{0:T(128)S(1)} %stack.88.scalars_ref, bf16[256,1024]{1,0:T(8,128)(2,1)S(1)} %copy-done.2, bf16[272,128]{1,0:T(8,128)(2,1)S(1)} %get-tuple-element.108.refs_0_, bf16[272,128]{1,0:T(8,128)(2,1)S(1)} %collective-permute-done.refs_1_, ...), custom_call_target="tpu_custom_call" | custom-call | flops 2147483648 | bytes 2097152 | tf_op jit(solution)/shard_map/attention/pallas_call | solution.py:93
  38.6 5.3 %project.2 = (bf16[2,128,1024]{2,1,0:T(8,128)(2,1)S(1)}, bf16[2,128,1024]{2,1,0:T(8,128)(2,1)S(1)}, bf16[2,128,1024]{2,1,0:T(8,128)(2,1)S(1)}, bf16[2,128,1024]{2,1,0:T(8,128)(2,1)S(1)}, f32[8,128]{1,0:T(8,128)S(1)}) custom-call(s32[3]{0:T(128)S(1)} %pad_add_fusion.refs_0_, bf16[256,1024]{1,0:T(8,128)(2,1)S(1)} %attention.1.refs_1_, ...), custom_call_target="tpu_custom_call" | custom-call | bytes 131072 | tf_op jit(solution)/shard_map/project/pallas_call | solution.py:124
  47.3 12.5 %project.3 = (bf16[2,128,1024]{2,1,0:T(8,128)(2,1)S(1)}, bf16[2,128,1024]{2,1,0:T(8,128)(2,1)S(1)}, bf16[2,128,1024]{2,1,0:T(8,128)(2,1)S(1)}, bf16[2,128,1024]{...) custom-call(s32[3]{0:T(128)S(1)} %pad_add_fusion.refs_0_, ...), custom_call_target="tpu_custom_call" | custom-call | bytes 131072 | tf_op jit(solution)/shard_map/project/pallas_call | solution.py:124
  62.4 5.8 %collective-permute-done.21.refs_5_ = bf16[128,1024]{1,0:T(8,128)(2,1)S(1)} collective-permute-done((bf16[128,1024]{1,0:T(8,128)(2,1)S(1)}, bf16[128,1024]{1,0:T(8,128)(2,1)S(1)}, u32[]{:S(2)}, u32[]{:S(2)}) %collective-permute-start.21) | collective-permute-done | bytes 262176 | tf_op jit(solution)/shard_map/ppermute | solution.py:316
  70.5 2.8 %collective-permute-start.26 = (bf16[128,1024]{1,0:T(8,128)(2,1)S(1)}, bf16[128,1024]{1,0:T(8,128)(2,1)S(1)}, u32[]{:S(2)}, u32[]{:S(2)}) collective-permute-start(bf16[128,1024]{1,0:T(8,128)(2,1)S(1)} %get-tuple-element.139), channel_id=1, source_target_pairs={{0,4},{1,5},{2,6},{3,7},{4,0},{5,1},{6,2},{7,3},{8,12},{9,13},{10,... | collective-permute-start | bytes 786440 | tf_op jit(solution)/shard_map/ppermute | solution.py:316
  77.3 2.6 %collective-permute-done.26.refs_6_ = bf16[128,1024]{1,0:T(8,128)(2,1)S(1)} collective-permute-done((bf16[128,1024]{1,0:T(8,128)(2,1)S(1)}, bf16[128,1024]{1,0:T(8,128)(2,1)S(1)}, u32[]{:S(2)}, u32[]{:S(2)}) %collective-permute-start.26) | collective-permute-done | bytes 262176 | tf_op jit(solution)/shard_map/ppermute | solution.py:316
  81.2 2.8 %collective-permute-start.17 = (bf16[2,128,1024]{2,1,0:T(8,128)(2,1)S(1)}, bf16[2,128,1024]{2,1,0:T(8,128)(2,1)S(1)}, u32[]{:S(2)}, u32[]{:S(2)}) collective-permute-start(bf16[2,128,1024]{2,1,0:T(8,128)(2,1)S(1)} %get-tuple-element.124), channel_id=1, source_target_pairs={{0,1},{1,0},{2,3},{3,2},{4,5},{5,4},{6,7},{7,6},{8,9},{9,8},{10,11... | collective-permute-start | bytes 1572872 | tf_op jit(solution)/shard_map/ppermute | solution.py:316
  84.9 2.8 %collective-permute-start.32 = (bf16[128,1024]{1,0:T(8,128)(2,1)S(1)}, bf16[128,1024]{1,0:T(8,128)(2,1)S(1)}, u32[]{:S(2)}, u32[]{:S(2)}) collective-permute-start(bf16[128,1024]{1,0:T(8,128)(2,1)S(1)} %get-tuple-element.148), channel_id=1, source_target_pairs={{0,4},{1,5},{2,6},{3,7},{4,0},{5,1},{6,2},{7,3},{8,12},{9,13},{10,... | collective-permute-start | bytes 786440 | tf_op jit(solution)/shard_map/ppermute | solution.py:316
  89.2 4.6 %collective-permute-start.28 = (bf16[128,1024]{1,0:T(8,128)(2,1)S(1)}, bf16[128,1024]{1,0:T(8,128)(2,1)S(1)}, u32[]{:S(2)}, u32[]{:S(2)}) collective-permute-start(bf16[128,1024]{1,0:T(8,128)(2,1)S(1)} %get-tuple-element.143), channel_id=1, source_target_pairs={{0,4},{1,5},{2,6},{3,7},{4,0},{5,1},{6,2},{7,3},{8,12},{9,13},{10,... | collective-permute-start | bytes 786440 | tf_op jit(solution)/shard_map/ppermute | solution.py:316
  96.6 3.7 %collective-permute-start.38 = (bf16[128,1024]{1,0:T(8,128)(2,1)S(1)}, bf16[128,1024]{1,0:T(8,128)(2,1)S(1)}, u32[]{:S(2)}, u32[]{:S(2)}) collective-permute-start(bf16[128,1024]{1,0:T(8,128)(2,1)S(1)} %get-tuple-element.156.refs_11_), channel_id=1, source_target_pairs={{0,4},{1,5},{2,6},{3,7},{4,0},{5,1},{6,2},{7,3},{8,12},{9,13},{10,... | collective-permute-start | bytes 786440 | tf_op jit(solution)/shard_map/ppermute | solution.py:316
  103.4 3.3 %collective-permute-start.36 = (bf16[128,1024]{1,0:T(8,128)(2,1)S(1)}, bf16[128,1024]{1,0:T(8,128)(2,1)S(1)}, u32[]{:S(2)}, u32[]{:S(2)}) collective-permute-start(bf16[128,1024]{1,0:T(8,128)(2,1)S(1)} %get-tuple-element.154.refs_11_), channel_id=1, source_target_pairs={{0,4},{1,5},{2,6},{3,7},{4,0},{5,1},{6,2},{7,3},{8,12},{9,13},{10,... | collective-permute-start | bytes 786440 | tf_op jit(solution)/shard_map/ppermute | solution.py:316
  108.2 2.4 %collective-permute-start.44 = (bf16[128,1024]{1,0:T(8,128)(2,1)S(1)}, bf16[128,1024]{1,0:T(8,128)(2,1)S(1)}, u32[]{:S(2)}, u32[]{:S(2)}) collective-permute-start(bf16[128,1024]{1,0:T(8,128)(2,1)S(1)} %get-tuple-element.164.refs_8_), channel_id=1, source_target_pairs={{0,4},{1,5},{2,6},{3,7},{4,0},{5,1},{6,2},{7,3},{8,12},{9,13},{10,... | collective-permute-start | bytes 786440 | tf_op jit(solution)/shard_map/ppermute | solution.py:316
  113.8 2.5 %collective-permute-start.41 = (bf16[128,1024]{1,0:T(8,128)(2,1)S(1)}, bf16[128,1024]{1,0:T(8,128)(2,1)S(1)}, u32[]{:S(2)}, u32[]{:S(2)}) collective-permute-start(bf16[128,1024]{1,0:T(8,128)(2,1)S(1)} %get-tuple-element.161.refs_8_), channel_id=1, source_target_pairs={{0,4},{1,5},{2,6},{3,7},{4,0},{5,1},{6,2},{7,3},{8,12},{9,13},{10,... | collective-permute-start | bytes 786440 | tf_op jit(solution)/shard_map/ppermute | solution.py:316
  119.4 6.3 %collective-permute-start.52 = (bf16[128,1024]{1,0:T(8,128)(2,1)S(1)}, bf16[128,1024]{1,0:T(8,128)(2,1)S(1)}, u32[]{:S(2)}, u32[]{:S(2)}) collective-permute-start(bf16[128,1024]{1,0:T(8,128)(2,1)S(1)} %get-tuple-element.174.refs_4_), channel_id=1, source_target_pairs={{0,4},{1,5},{2,6},{3,7},{4,0},{5,1},{6,2},{7,3},{8,12},{9,13},{10,... | collective-permute-start | bytes 786440 | tf_op jit(solution)/shard_map/ppermute | solution.py:316
  125.7 6.8 %collective-permute-start.50 = (bf16[2,128,1024]{2,1,0:T(8,128)(2,1)S(1)}, bf16[2,128,1024]{2,1,0:T(8,128)(2,1)S(1)}, u32[]{:S(2)}, u32[]{:S(2)}) collective-permute-start(bf16[2,128,1024]{2,1,0:T(8,128)(2,1)S(1)} %get-tuple-element.172.refs_1_), channel_id=1, source_target_pairs={{0,1},{1,0},{2,3},{3,2},{4,5},{5,4},{6,7},{7,6},{8,9},{9,8},{10,11... | collective-permute-start | bytes 1572872 | tf_op jit(solution)/shard_map/ppermute | solution.py:316
  134.2 3.6 %collective-permute-start.48 = (bf16[128,1024]{1,0:T(8,128)(2,1)S(1)}, bf16[128,1024]{1,0:T(8,128)(2,1)S(1)}, u32[]{:S(2)}, u32[]{:S(2)}) collective-permute-start(bf16[128,1024]{1,0:T(8,128)(2,1)S(1)} %get-tuple-element.170.refs_4_), channel_id=1, source_target_pairs={{0,4},{1,5},{2,6},{3,7},{4,0},{5,1},{6,2},{7,3},{8,12},{9,13},{10,... | collective-permute-start | bytes 786440 | tf_op jit(solution)/shard_map/ppermute | solution.py:316
  137.8 2.6 %collective-permute-done.53.refs_6_ = bf16[128,1024]{1,0:T(8,128)(2,1)S(1)} collective-permute-done((bf16[128,1024]{1,0:T(8,128)(2,1)S(1)}, bf16[128,1024]{1,0:T(8,128)(2,1)S(1)}, u32[]{:S(2)}, u32[]{:S(2)}) %collective-permute-start.53) | collective-permute-done | bytes 262176 | tf_op jit(solution)/shard_map/ppermute | solution.py:316
  141.9 4.7 %collective-permute-start.56 = (bf16[2,128,1024]{2,1,0:T(8,128)(2,1)S(1)}, bf16[2,128,1024]{2,1,0:T(8,128)(2,1)S(1)}, u32[]{:S(2)}, u32[]{:S(2)}) collective-permute-start(bf16[2,128,1024]{2,1,0:T(8,128)(2,1)S(1)} %get-tuple-element.181.refs_1_), channel_id=1, source_target_pairs={{0,1},{1,0},{2,3},{3,2},{4,5},{5,4},{6,7},{7,6},{8,9},{9,8},{10,11... | collective-permute-start | bytes 1572872 | tf_op jit(solution)/shard_map/ppermute | solution.py:316
  158.2 3.0 %collective-permute-done.55.refs_4_ = bf16[128,1024]{1,0:T(8,128)(2,1)S(1)} collective-permute-done((bf16[128,1024]{1,0:T(8,128)(2,1)S(1)}, bf16[128,1024]{1,0:T(8,128)(2,1)S(1)}, u32[]{:S(2)}, u32[]{:S(2)}) %collective-permute-start.55) | collective-permute-done | bytes 262176 | tf_op jit(solution)/shard_map/ppermute | solution.py:316
  170.1 2.4 %collective-permute-done.60.refs_2_ = bf16[128,1024]{1,0:T(8,128)(2,1)S(1)} collective-permute-done((bf16[128,1024]{1,0:T(8,128)(2,1)S(1)}, bf16[128,1024]{1,0:T(8,128)(2,1)S(1)}, u32[]{:S(2)}, u32[]{:S(2)}) %collective-permute-start.60) | collective-permute-done | bytes 262176 | tf_op jit(solution)/shard_map/ppermute | solution.py:316
  (151 shorter events, 69.1 us)
Async XLA Ops:
  11.1 15.3 %collective-permute-start.5 = (bf16[272,128]{1,0:T(8,128)(2,1)S(1)}, bf16[272,128]{1,0:T(8,128)(2,1)S(1)}, u32[]{:S(2)}, u32[]{:S(2)}) collective-permute-start(bf16[272,128]{1,0:T(8,128)(2,1)S(1)} %get-tuple-element.111), channel_id=1, source_target_pairs={{0,10},{1,11},{2,8},{3,9},{4,14},{5,15},{6,12},{7,13},{8,2},{9,3},... | collective-permute-start | bytes 208904 | tf_op jit(solution)/shard_map/ppermute | solution.py:316
  11.5 14.9 %collective-permute-start.7 = (bf16[272,128]{1,0:T(8,128)(2,1)S(1)}, bf16[272,128]{1,0:T(8,128)(2,1)S(1)}, u32[]{:S(2)}, u32[]{:S(2)}) collective-permute-start(bf16[272,128]{1,0:T(8,128)(2,1)S(1)} %get-tuple-element.112), channel_id=1, source_target_pairs={{0,8},{1,9},{2,10},{3,11},{4,12},{5,13},{6,14},{7,15},{8,0},{9,1},... | collective-permute-start | bytes 208904 | tf_op jit(solution)/shard_map/ppermute | solution.py:316
  13.5 13.5 %collective-permute-start = (bf16[272,128]{1,0:T(8,128)(2,1)S(1)}, bf16[272,128]{1,0:T(8,128)(2,1)S(1)}, u32[]{:S(2)}, u32[]{:S(2)}) collective-permute-start(bf16[272,128]{1,0:T(8,128)(2,1)S(1)} %get-tuple-element.108.refs_0_), channel_id=1, source_target_pairs={{0,1},{1,0},{2,3},{3,2},{4,5},{5,4},{6,7},{7,6},{8,9},{9,8},{10,11... | collective-permute-start | bytes 208904 | tf_op jit(solution)/shard_map/ppermute | solution.py:316
  15.8 11.2 %collective-permute-start.10 = (bf16[272,128]{1,0:T(8,128)(2,1)S(1)}, bf16[272,128]{1,0:T(8,128)(2,1)S(1)}, u32[]{:S(2)}, u32[]{:S(2)}) collective-permute-start(bf16[272,128]{1,0:T(8,128)(2,1)S(1)} %collective-permute-done.9.refs_10_), channel_id=1, source_target_pairs={{0,1},{1,0},{2,3},{3,2},{4,5},{5,4},{6,7},{7,6},{8,9},{9,8},{10,11... | collective-permute-start | bytes 208904 | tf_op jit(solution)/shard_map/ppermute | solution.py:316
  16.1 11.3 %collective-permute-start.12 = (bf16[272,128]{1,0:T(8,128)(2,1)S(1)}, bf16[272,128]{1,0:T(8,128)(2,1)S(1)}, u32[]{:S(2)}, u32[]{:S(2)}) collective-permute-start(bf16[272,128]{1,0:T(8,128)(2,1)S(1)} %collective-permute-done.11.refs_12_), channel_id=1, source_target_pairs={{0,1},{1,0},{2,3},{3,2},{4,5},{5,4},{6,7},{7,6},{8,9},{9,8},{10,11... | collective-permute-start | bytes 208904 | tf_op jit(solution)/shard_map/ppermute | solution.py:316
  60.1 14.0 %collective-permute-start.18 = (bf16[2,128,1024]{2,1,0:T(8,128)(2,1)S(1)}, bf16[2,128,1024]{2,1,0:T(8,128)(2,1)S(1)}, u32[]{:S(2)}, u32[]{:S(2)}) collective-permute-start(bf16[2,128,1024]{2,1,0:T(8,128)(2,1)S(1)} %get-tuple-element.126), channel_id=1, source_target_pairs={{0,1},{1,0},{2,3},{3,2},{4,5},{5,4},{6,7},{7,6},{8,9},{9,8},{10,11... | collective-permute-start | bytes 1572872 | tf_op jit(solution)/shard_map/ppermute | solution.py:316
  60.5 15.3 %collective-permute-start.25 = (bf16[2,128,1024]{2,1,0:T(8,128)(2,1)S(1)}, bf16[2,128,1024]{2,1,0:T(8,128)(2,1)S(1)}, u32[]{:S(2)}, u32[]{:S(2)}) collective-permute-start(bf16[2,128,1024]{2,1,0:T(8,128)(2,1)S(1)} %get-tuple-element.138), channel_id=1, source_target_pairs={{0,1},{1,0},{2,3},{3,2},{4,5},{5,4},{6,7},{7,6},{8,9},{9,8},{10,11... | collective-permute-start | bytes 1572872 | tf_op jit(solution)/shard_map/ppermute | solution.py:316
  60.6 13.2 %collective-permute-start.19 = (bf16[128,1024]{1,0:T(8,128)(2,1)S(1)}, bf16[128,1024]{1,0:T(8,128)(2,1)S(1)}, u32[]{:S(2)}, u32[]{:S(2)}) collective-permute-start(bf16[128,1024]{1,0:T(8,128)(2,1)S(1)} %get-tuple-element.127), channel_id=1, source_target_pairs={{0,2},{1,3},{2,0},{3,1},{4,6},{5,7},{6,4},{7,5},{8,10},{9,11},{10,... | collective-permute-start | bytes 786440 | tf_op jit(solution)/shard_map/ppermute | solution.py:316
  68.2 16.7 %collective-permute-start.23 = (bf16[2,128,1024]{2,1,0:T(8,128)(2,1)S(1)}, bf16[2,128,1024]{2,1,0:T(8,128)(2,1)S(1)}, u32[]{:S(2)}, u32[]{:S(2)}) collective-permute-start(bf16[2,128,1024]{2,1,0:T(8,128)(2,1)S(1)} %get-tuple-element.135), channel_id=1, source_target_pairs={{0,1},{1,0},{2,3},{3,2},{4,5},{5,4},{6,7},{7,6},{8,9},{9,8},{10,11... | collective-permute-start | bytes 1572872 | tf_op jit(solution)/shard_map/ppermute | solution.py:316
  74.1 15.1 %collective-permute-start.31 = (bf16[2,128,1024]{2,1,0:T(8,128)(2,1)S(1)}, bf16[2,128,1024]{2,1,0:T(8,128)(2,1)S(1)}, u32[]{:S(2)}, u32[]{:S(2)}) collective-permute-start(bf16[2,128,1024]{2,1,0:T(8,128)(2,1)S(1)} %get-tuple-element.147), channel_id=1, source_target_pairs={{0,1},{1,0},{2,3},{3,2},{4,5},{5,4},{6,7},{7,6},{8,9},{9,8},{10,11... | collective-permute-start | bytes 1572872 | tf_op jit(solution)/shard_map/ppermute | solution.py:316
  75.8 11.9 %collective-permute-start.22 = (bf16[128,1024]{1,0:T(8,128)(2,1)S(1)}, bf16[128,1024]{1,0:T(8,128)(2,1)S(1)}, u32[]{:S(2)}, u32[]{:S(2)}) collective-permute-start(bf16[128,1024]{1,0:T(8,128)(2,1)S(1)} %get-tuple-element.133), channel_id=1, source_target_pairs={{0,2},{1,3},{2,0},{3,1},{4,6},{5,7},{6,4},{7,5},{8,10},{9,11},{10,... | collective-permute-start | bytes 786440 | tf_op jit(solution)/shard_map/ppermute | solution.py:316
  81.2 19.2 %collective-permute-start.17 = (bf16[2,128,1024]{2,1,0:T(8,128)(2,1)S(1)}, bf16[2,128,1024]{2,1,0:T(8,128)(2,1)S(1)}, u32[]{:S(2)}, u32[]{:S(2)}) collective-permute-start(bf16[2,128,1024]{2,1,0:T(8,128)(2,1)S(1)} %get-tuple-element.124), channel_id=1, source_target_pairs={{0,1},{1,0},{2,3},{3,2},{4,5},{5,4},{6,7},{7,6},{8,9},{9,8},{10,11... | collective-permute-start | bytes 1572872 | tf_op jit(solution)/shard_map/ppermute | solution.py:316
  89.2 12.4 %collective-permute-start.28 = (bf16[128,1024]{1,0:T(8,128)(2,1)S(1)}, bf16[128,1024]{1,0:T(8,128)(2,1)S(1)}, u32[]{:S(2)}, u32[]{:S(2)}) collective-permute-start(bf16[128,1024]{1,0:T(8,128)(2,1)S(1)} %get-tuple-element.143), channel_id=1, source_target_pairs={{0,4},{1,5},{2,6},{3,7},{4,0},{5,1},{6,2},{7,3},{8,12},{9,13},{10,... | collective-permute-start | bytes 786440 | tf_op jit(solution)/shard_map/ppermute | solution.py:316
  113.8 11.9 %collective-permute-start.41 = (bf16[128,1024]{1,0:T(8,128)(2,1)S(1)}, bf16[128,1024]{1,0:T(8,128)(2,1)S(1)}, u32[]{:S(2)}, u32[]{:S(2)}) collective-permute-start(bf16[128,1024]{1,0:T(8,128)(2,1)S(1)} %get-tuple-element.161.refs_8_), channel_id=1, source_target_pairs={{0,4},{1,5},{2,6},{3,7},{4,0},{5,1},{6,2},{7,3},{8,12},{9,13},{10,... | collective-permute-start | bytes 786440 | tf_op jit(solution)/shard_map/ppermute | solution.py:316
  116.3 16.2 %collective-permute-start.42 = (bf16[128,1024]{1,0:T(8,128)(2,1)S(1)}, bf16[128,1024]{1,0:T(8,128)(2,1)S(1)}, u32[]{:S(2)}, u32[]{:S(2)}) collective-permute-start(bf16[128,1024]{1,0:T(8,128)(2,1)S(1)} %get-tuple-element.162.refs_5_), channel_id=1, source_target_pairs={{4,8},{5,9},{6,10},{7,11},{8,4},{9,5},{10,6},{11,7},{20,24},{21,25... | collective-permute-start | bytes 786440 | tf_op jit(solution)/shard_map/ppermute | solution.py:320
  117.5 15.0 %collective-permute-start.43 = (bf16[128,1024]{1,0:T(8,128)(2,1)S(1)}, bf16[128,1024]{1,0:T(8,128)(2,1)S(1)}, u32[]{:S(2)}, u32[]{:S(2)}) collective-permute-start(bf16[128,1024]{1,0:T(8,128)(2,1)S(1)} %get-tuple-element.163.refs_9_), channel_id=1, source_target_pairs={{0,2},{1,3},{2,0},{3,1},{4,6},{5,7},{6,4},{7,5},{8,10},{9,11},{10,... | collective-permute-start | bytes 786440 | tf_op jit(solution)/shard_map/ppermute | solution.py:316
  118.7 14.8 %collective-permute-start.51 = (bf16[128,1024]{1,0:T(8,128)(2,1)S(1)}, bf16[128,1024]{1,0:T(8,128)(2,1)S(1)}, u32[]{:S(2)}, u32[]{:S(2)}) collective-permute-start(bf16[128,1024]{1,0:T(8,128)(2,1)S(1)} %get-tuple-element.173.refs_1_), channel_id=1, source_target_pairs={{4,8},{5,9},{6,10},{7,11},{8,4},{9,5},{10,6},{11,7},{20,24},{21,25... | collective-permute-start | bytes 786440 | tf_op jit(solution)/shard_map/ppermute | solution.py:320
  119.4 14.8 %collective-permute-start.52 = (bf16[128,1024]{1,0:T(8,128)(2,1)S(1)}, bf16[128,1024]{1,0:T(8,128)(2,1)S(1)}, u32[]{:S(2)}, u32[]{:S(2)}) collective-permute-start(bf16[128,1024]{1,0:T(8,128)(2,1)S(1)} %get-tuple-element.174.refs_4_), channel_id=1, source_target_pairs={{0,4},{1,5},{2,6},{3,7},{4,0},{5,1},{6,2},{7,3},{8,12},{9,13},{10,... | collective-permute-start | bytes 786440 | tf_op jit(solution)/shard_map/ppermute | solution.py:316
  125.7 20.9 %collective-permute-start.50 = (bf16[2,128,1024]{2,1,0:T(8,128)(2,1)S(1)}, bf16[2,128,1024]{2,1,0:T(8,128)(2,1)S(1)}, u32[]{:S(2)}, u32[]{:S(2)}) collective-permute-start(bf16[2,128,1024]{2,1,0:T(8,128)(2,1)S(1)} %get-tuple-element.172.refs_1_), channel_id=1, source_target_pairs={{0,1},{1,0},{2,3},{3,2},{4,5},{5,4},{6,7},{7,6},{8,9},{9,8},{10,11... | collective-permute-start | bytes 1572872 | tf_op jit(solution)/shard_map/ppermute | solution.py:316
  133.3 17.7 %collective-permute-start.57 = (bf16[2,128,1024]{2,1,0:T(8,128)(2,1)S(1)}, bf16[2,128,1024]{2,1,0:T(8,128)(2,1)S(1)}, u32[]{:S(2)}, u32[]{:S(2)}) collective-permute-start(bf16[2,128,1024]{2,1,0:T(8,128)(2,1)S(1)} %get-tuple-element.182.refs_1_), channel_id=1, source_target_pairs={{0,1},{1,0},{2,3},{3,2},{4,5},{5,4},{6,7},{7,6},{8,9},{9,8},{10,11... | collective-permute-start | bytes 1572872 | tf_op jit(solution)/shard_map/ppermute | solution.py:316
  141.2 11.9 %collective-permute-start.58 = (bf16[128,1024]{1,0:T(8,128)(2,1)S(1)}, bf16[128,1024]{1,0:T(8,128)(2,1)S(1)}, u32[]{:S(2)}, u32[]{:S(2)}) collective-permute-start(bf16[128,1024]{1,0:T(8,128)(2,1)S(1)} %get-tuple-element.186.refs_2_), channel_id=1, source_target_pairs={{0,4},{1,5},{2,6},{3,7},{4,0},{5,1},{6,2},{7,3},{8,12},{9,13},{10,... | collective-permute-start | bytes 786440 | tf_op jit(solution)/shard_map/ppermute | solution.py:316
  141.9 14.1 %collective-permute-start.56 = (bf16[2,128,1024]{2,1,0:T(8,128)(2,1)S(1)}, bf16[2,128,1024]{2,1,0:T(8,128)(2,1)S(1)}, u32[]{:S(2)}, u32[]{:S(2)}) collective-permute-start(bf16[2,128,1024]{2,1,0:T(8,128)(2,1)S(1)} %get-tuple-element.181.refs_1_), channel_id=1, source_target_pairs={{0,1},{1,0},{2,3},{3,2},{4,5},{5,4},{6,7},{7,6},{8,9},{9,8},{10,11... | collective-permute-start | bytes 1572872 | tf_op jit(solution)/shard_map/ppermute | solution.py:316
  151.1 13.7 %collective-permute-start.62 = (bf16[2,128,1024]{2,1,0:T(8,128)(2,1)S(1)}, bf16[2,128,1024]{2,1,0:T(8,128)(2,1)S(1)}, u32[]{:S(2)}, u32[]{:S(2)}) collective-permute-start(bf16[2,128,1024]{2,1,0:T(8,128)(2,1)S(1)} %get-tuple-element.193.refs_1_), channel_id=1, source_target_pairs={{0,1},{1,0},{2,3},{3,2},{4,5},{5,4},{6,7},{7,6},{8,9},{9,8},{10,11... | collective-permute-start | bytes 1572872 | tf_op jit(solution)/shard_map/ppermute | solution.py:316
  155.4 13.2 %collective-permute-start.61 = (bf16[2,128,1024]{2,1,0:T(8,128)(2,1)S(1)}, bf16[2,128,1024]{2,1,0:T(8,128)(2,1)S(1)}, u32[]{:S(2)}, u32[]{:S(2)}) collective-permute-start(bf16[2,128,1024]{2,1,0:T(8,128)(2,1)S(1)} %get-tuple-element.192.refs_1_), channel_id=1, source_target_pairs={{0,1},{1,0},{2,3},{3,2},{4,5},{5,4},{6,7},{7,6},{8,9},{9,8},{10,11... | collective-permute-start | bytes 1572872 | tf_op jit(solution)/shard_map/ppermute | solution.py:316
  (46 other events, 301.0 us)

commit v2 on v1

v2 whole, which is shorter than its diff:
```python
import functools
import math

import jax
import jax.numpy as jnp
from jax import lax
from jax.experimental import pallas as pl
from jax.experimental.pallas import tpu as pltpu
from jax.sharding import PartitionSpec as P

HEADS = 128
KV_HEADS = 8
HEAD_DIM = 128
GROUP = HEADS // KV_HEADS
FLAG_ROWS = 16
CHUNKS = 8
BLOCK_COLS = 512
SLOTS = 8
VMEM_LIMIT = 32 * 1024 * 1024
PACK_VMEM_LIMIT = 56 * 1024 * 1024
ATTENTION_ROWS = 256


def position():
    me = lax.axis_index("tensor")
    core, chip = lax.rem(me, 2), lax.div(me, 2)
    return core, chip, lax.rem(chip, 2), lax.div(chip, 2)


def pack_kernel(local_heads, lengths_ref, q_ref, k_ref, v_ref, q_out, *refs):
    out_refs, sems = refs[:-1], refs[-1]
    slots = k_ref.shape[0]
    _, chip, _, _ = position()
    copies = []
    for m in reversed(range(len(out_refs))):
        head = lax.div((chip ^ m) * (2 * local_heads), GROUP)
        cols = pl.ds(pl.multiple_of(head * HEAD_DIM, HEAD_DIM), HEAD_DIM)
        for i, ref in enumerate((k_ref, v_ref)):
            rows = pl.ds(i * slots, slots)
            copies.append(
                pltpu.make_async_copy(ref.at[:, cols], out_refs[m].at[rows], sems.at[2 * m + i])
            )
            copies[-1].start()
    copies.append(pltpu.make_async_copy(q_ref, q_out, sems.at[2 * len(out_refs)]))
    copies[-1].start()
    length = jnp.full((FLAG_ROWS, HEAD_DIM), lengths_ref[0], jnp.int32)
    length = length.astype(jnp.float32).astype(jnp.bfloat16)
    for out in out_refs:
        out[2 * slots :, :] = length
    for copy in copies:
        copy.wait()


def pack(chips, local_heads, lengths, queries, keys, values):
    slots = keys.shape[0]
    piece = jax.ShapeDtypeStruct((2 * slots + FLAG_ROWS, HEAD_DIM), jnp.bfloat16)
    return pl.pallas_call(
        functools.partial(pack_kernel, local_heads),
        out_shape=[jax.ShapeDtypeStruct(queries.shape, queries.dtype)] + [piece] * chips,
        in_specs=[SMEM, ANY, ANY, ANY],
        out_specs=[VMEM] * (1 + chips),
        scratch_shapes=[pltpu.SemaphoreType.DMA((2 * chips + 1,))],
        compiler_params=pltpu.CompilerParams(vmem_limit_bytes=PACK_VMEM_LIMIT),
        name="pack_kv",
    )(lengths, queries, keys, values)


def bundle_kernel(*refs):
    for i, ref in enumerate(refs[:-1]):
        refs[-1][i] = ref[...]


def bundle(turn, pieces):
    shape = (len(pieces), *pieces[0].shape)
    (out,), turn = call(
        bundle_kernel,
        turn,
        pieces,
        [VMEM] * len(pieces),
        [jax.ShapeDtypeStruct(shape, pieces[0].dtype)],
        [VMEM],
        "bundle",
    )
    return out, turn


def attention_kernel(flip, start_ref, queries, pieces, *refs):
    last = flip == 1
    if last:
        near, near_top, near_total, out_ref, *refs = refs
    else:
        near, near_top, near_total, *refs = refs
    keys, values, bias = refs
    tokens = queries.shape[0]
    half = tokens // 2
    slots = (pieces.shape[1] - FLAG_ROWS) // 2
    core, chip, _, _ = position()
    token = lax.broadcasted_iota(jnp.int32, (tokens, slots), 0) + start_ref[0]
    lane = lax.broadcasted_iota(jnp.int32, (tokens, slots), 1)
    lane_row = lax.broadcasted_iota(jnp.int32, (1, slots), 1).astype(jnp.float32)
    for m in range(pieces.shape[0]):
        rows = slice(m * slots, (m + 1) * slots)
        keys[rows, :] = pieces[m, :slots, :]
        values[rows, :] = pieces[m, slots : 2 * slots, :]
        length = pieces[m, 2 * slots :, :].astype(jnp.float32)[:1, :slots]
        dead = jnp.where(lane_row < length, 0.0, -1e30)
        shard = (chip ^ m) * 2 + (core ^ flip)
        bias[:, rows] = jnp.where(lane + shard * slots <= token, dead, -1e30)
    factor = HEAD_DIM ** (-0.5) * math.log2(math.e)
    for head in range(queries.shape[1] // HEAD_DIM):
        cols = slice(head * HEAD_DIM, (head + 1) * HEAD_DIM)
        for block in range(tokens // ATTENTION_ROWS):
            rows = slice(block * ATTENTION_ROWS, (block + 1) * ATTENTION_ROWS)
            scores = lax.dot_general(
                queries[rows, cols],
                keys[...],
                (((1,), (1,)), ((), ())),
                preferred_element_type=jnp.float32,
            )
            scores = scores + bias[rows, :]
            top = jnp.max(scores, axis=-1, keepdims=True)
            if last:
                top_before = near_top[rows, head : head + 1]
                top = jnp.maximum(top, top_before)
            weights = jnp.exp2((scores - top) * factor)
            total = jnp.sum(weights, axis=-1, keepdims=True)
            mixed = jnp.dot(
                weights.astype(jnp.bfloat16), values[...], preferred_element_type=jnp.float32
            )
            if last:
                shrink = jnp.exp2((top_before - top) * factor)
                total = total + near_total[rows, head : head + 1] * shrink
                mixed = mixed + near[rows, cols] * shrink
                result = (mixed / total).astype(jnp.bfloat16)
                for i in range(0, ATTENTION_ROWS, min(half, ATTENTION_ROWS)):
                    first = block * ATTENTION_ROWS + i
                    first = first + core * jnp.where(first < half, half, -half)
                    place = pl.ds(pl.multiple_of(first, 128), min(half, ATTENTION_ROWS))
                    out_ref[place, cols] = result[i : i + min(half, ATTENTION_ROWS)]
            else:
                near[rows, cols] = mixed
                near_top[rows, head : head + 1] = top
                near_total[rows, head : head + 1] = total


def attention(turn, start_pos, queries, pieces, flip, before=None):
    tokens, width = queries.shape
    count = pieces.shape[0]
    slots = (pieces.shape[1] - FLAG_ROWS) // 2
    heads = width // HEAD_DIM
    last = before is not None
    sums = [
        jax.ShapeDtypeStruct((tokens, width), jnp.float32),
        jax.ShapeDtypeStruct((tokens, heads), jnp.float32),
        jax.ShapeDtypeStruct((tokens, heads), jnp.float32),
    ]
    given = before if last else []
    outs = [jax.ShapeDtypeStruct((tokens, width), jnp.bfloat16)] if last else sums
    return call(
        functools.partial(attention_kernel, flip),
        turn,
        [start_pos, queries, pieces, *given],
        [SMEM] + [VMEM] * (2 + len(given)),
        outs,
        [VMEM] * len(outs),
        "attention_theirs" if last else "attention_mine",
        [
            pltpu.VMEM((count * slots, HEAD_DIM), jnp.bfloat16),
            pltpu.VMEM((count * slots, HEAD_DIM), jnp.bfloat16),
            pltpu.VMEM((tokens, count * slots), jnp.float32),
        ],
        bytes_accessed=1 << 24,
    )


VMEM = pl.BlockSpec(memory_space=pltpu.VMEM)
SMEM = pl.BlockSpec(memory_space=pltpu.SMEM)
ANY = pl.BlockSpec(memory_space=pl.ANY)


def in_order(kernel, ins, outs):
    def body(*refs):
        inputs, rest = refs[:ins], refs[ins + 1 :]
        kernel(*inputs, *rest[:outs], *rest[outs + 1 :])
        rest[outs][...] = jnp.zeros_like(rest[outs])

    return body


def call(kernel, turn, args, in_specs, out_shapes, out_specs, name, scratch=(), aliases=None, bytes_accessed=1 << 17):
    turn_shape = jax.ShapeDtypeStruct((8, 128), jnp.float32)
    *results, turn = pl.pallas_call(
        in_order(kernel, len(args), len(out_shapes)),
        out_shape=[*out_shapes, turn_shape],
        in_specs=[*in_specs, pl.BlockSpec(memory_space=pl.ANY)],
        out_specs=[*out_specs, VMEM],
        scratch_shapes=list(scratch),
        input_output_aliases=aliases or {},
        compiler_params=pltpu.CompilerParams(vmem_limit_bytes=VMEM_LIMIT),
        cost_estimate=pl.CostEstimate(flops=0, bytes_accessed=bytes_accessed, transcendentals=0),
        name=name,
    )(*args, turn)
    return results, turn


def project_kernel(bases, width, a_ref, w_ref, *refs):
    outs, (buffer, sems) = refs[:-2], refs[-2:]
    half = a_ref.shape[0] // 2
    _, _, side, _ = position()
    tile = min(width, BLOCK_COLS)
    blocks = [
        (number, part, i)
        for number in range(len(bases))
        for part in range(2)
        for i in range(width // tile)
    ]
    copies = []
    for at, (number, part, i) in enumerate(blocks):
        first = bases[number] + (side ^ (1 - part)) * width + i * tile
        cols = pl.ds(pl.multiple_of(first, tile), tile)
        slot = at % buffer.shape[0]
        copies.append(pltpu.make_async_copy(w_ref.at[:, cols], buffer.at[slot], sems.at[slot]))
    for copy in copies[: buffer.shape[0]]:
        copy.start()
    for at, (number, part, i) in enumerate(blocks):
        copies[at].wait()
        product = jnp.dot(
            a_ref[...], buffer[at % buffer.shape[0]], preferred_element_type=jnp.float32
        ).astype(jnp.bfloat16)
        if at + buffer.shape[0] < len(blocks):
            copies[at + buffer.shape[0]].start()
        cols = slice(i * tile, (i + 1) * tile)
        outs[4 * number + part][:, cols] = product[:half]
        outs[4 * number + 2 + part][:, cols] = product[half:]


def project(turn, attended, weight, bases, width):
    tokens, depth = attended.shape
    out = jax.ShapeDtypeStruct((tokens // 2, width), jnp.bfloat16)
    count = 4 * len(bases)
    tile = min(width, BLOCK_COLS)
    slots = min(SLOTS, 2 * len(bases) * width // tile)
    return call(
        functools.partial(project_kernel, bases, width),
        turn,
        [attended, weight],
        [VMEM, ANY],
        [out] * count,
        [VMEM] * count,
        "project",
        [pltpu.VMEM((slots, depth, tile), jnp.bfloat16), pltpu.SemaphoreType.DMA((slots,))],
    )


def plus(*terms):
    total = terms[0].astype(jnp.float32)
    for term in terms[1:]:
        total = total + term.astype(jnp.float32)
    return total.astype(jnp.bfloat16)


def leave(own, core, out):
    out[...] = plus(own[...], core[...])


def join(own, core, beside, out):
    out[...] = plus(own[...], core[...], beside[...])


def inward(own, core, beside, near, out):
    out[...] = plus(own[...], core[...], beside[...], near[...])


def middle(own, across, out):
    out[...] = plus(own[...], across[...])


def is_inner():
    _, _, _, spot = position()
    return (spot == 1) | (spot == 2)


def join_and_middle(own, core, beside, near, across, out):
    inner = is_inner()

    @pl.when(jnp.logical_not(inner))
    def _():
        join(own, core, beside, out)

    @pl.when(inner)
    def _():
        middle(near, across, out)


def choose(near, own, out):
    inner = is_inner()

    @pl.when(jnp.logical_not(inner))
    def _():
        out[...] = near[...]

    @pl.when(inner)
    def _():
        out[...] = own[...]


def stack(own, beside, out):
    out[0] = own[...]
    out[1] = beside[...]


def tick_kernel(jobs, *refs):
    at = sum(len(ins) for _, ins, _ in jobs)
    outs = refs[at:]
    at = 0
    for (job, ins, _), out in zip(jobs, outs):
        job(*refs[at : at + len(ins)], out)
        at += len(ins)


def tick(turn, jobs):
    arrays = [x for _, ins, _ in jobs for x in ins]
    outs = [jax.ShapeDtypeStruct(shape, jnp.bfloat16) for _, _, shape in jobs]
    return call(
        functools.partial(tick_kernel, jobs),
        turn,
        arrays,
        [VMEM] * len(arrays),
        outs,
        [VMEM] * len(outs),
        "tick",
    )


def place_kernel(base, width, mine, theirs, *refs):
    out_ref, sems = refs[-2:]
    half = mine.shape[1]
    core, _, side, _ = position()
    copies = []
    for i in range(4):
        row = pl.multiple_of((core ^ (i // 2)) * half, half)
        col = pl.multiple_of(base + (side ^ (i % 2)) * width, width)
        source = (mine, theirs)[i // 2].at[i % 2]
        copies.append(
            pltpu.make_async_copy(
                source, out_ref.at[pl.ds(row, half), pl.ds(col, width)], sems.at[i]
            )
        )
    for copy in copies:
        copy.start()
    for copy in copies:
        copy.wait()


def place(turn, mine, theirs, out, base, shape):
    width = mine.shape[2]
    given = [] if out is None else [out]
    (out,), turn = call(
        functools.partial(place_kernel, base, width),
        turn,
        [mine, theirs, *given],
        [ANY, ANY] + [ANY] * len(given),
        [jax.ShapeDtypeStruct(shape, jnp.bfloat16)],
        [ANY],
        "place",
        [pltpu.SemaphoreType.DMA((4,))],
        {2: 0} if given else None,
    )
    return out, turn


def shards(devices, queries, keys, values, lengths, start_pos, out_weight):
    slots = keys.shape[0]
    tokens = queries.shape[0]
    columns = out_weight.shape[1]
    local_heads = queries.shape[1] // HEAD_DIM
    chips = devices // 2
    line = chips // 2

    def swap(x, bits):
        return lax.ppermute(x, "tensor", [(d, d ^ bits) for d in range(devices)])

    def along(x, pairs):
        perm = [(a * 4 + i, b * 4 + i) for a, b in pairs for i in range(4)]
        return lax.ppermute(x, "tensor", perm)

    turn = jnp.zeros((8, 128), jnp.float32)
    fetched, *packed = pack(chips, local_heads, lengths, queries, keys, values)
    direct = {m: swap(packed[m], 2 * m) if m else packed[0] for m in reversed(range(chips))}
    mine, turn = bundle(turn, [direct[m] for m in range(chips)])
    theirs = swap(mine, 1)
    sums, turn = attention(turn, start_pos, fetched, mine, 0)
    (attended,), turn = attention(turn, start_pos, fetched, theirs, 1, sums)

    if line != 4:
        partial_value = jnp.dot(attended, out_weight, preferred_element_type=jnp.float32)
        partial_value = jnp.roll(partial_value.astype(jnp.bfloat16), position()[0] * (tokens // 2), axis=0)
        summed = lax.psum_scatter(partial_value, "tensor", scatter_dimension=0, tiled=True)
        return lax.all_gather(summed, "tensor", axis=0, tiled=True)

    width = columns // (2 * CHUNKS)
    shape = (tokens // 2, width)
    chunks = [{"base": 2 * chunk * width} for chunk in range(CHUNKS)]
    out = None

    def project_some(turn, some):
        results, turn = project(
            turn, attended, out_weight, [c["base"] for c in some], width
        )
        for i, c in enumerate(some):
            c["own"] = results[4 * i : 4 * i + 2]
            c["core"] = [swap(peer, 1) for peer in results[4 * i + 2 : 4 * i + 4]]
        return turn

    def leave_of(c):
        return (leave, [c["own"][0], c["core"][0]], shape), [c], "beside", lambda x: swap(x, 2)

    def jobs_of(at):
        jobs = []
        if 4 in at:
            c = at[4]
            job = choose, [c["near"], c["near_sent"]], shape
            jobs.append((job, [c], "beside", lambda x: swap(x, 2)))
        early, late = at.get(1), at.get(3)
        if early or late:
            ins = [early["own"][1], early["core"][1], early["beside"]] if early else []
            ins += [late["across_sent"], late["across"]] if late else []
            job = join_and_middle if early and late else join if early else middle
            owners = [c for c in (early, late) if c]
            jobs.append(((job, ins, shape), owners, "near", lambda x: swap(x, 4)))
        if 2 in at:
            c = at[2]
            job = inward, [c["own"][1], c["core"][1], c["beside"], c["near"]], shape
            jobs.append((job, [c], "across", lambda x: along(x, [(1, 2), (2, 1)])))
        if 5 in at:
            c = at[5]
            job = stack, [c["beside_sent"], c["beside"]], (2, *shape)
            jobs.append((job, [c], "theirs", lambda x: swap(x, 1)))
        return jobs

    def run(turn, now):
        if not now:
            return turn
        results, turn = tick(turn, [job for job, _, _, _ in now])
        for (_, owners, key, send), x in zip(now, results):
            got = send(x)
            for c in owners:
                c[key], c[key + "_sent"] = got, x
        return turn

    lanes = [chunks[0::2], chunks[1::2]]
    turn = project_some(turn, chunks[:2])
    for time in range(len(lanes[0]) + 6):
        for lane in lanes:
            turn = run(turn, jobs_of({time - i: c for i, c in enumerate(lane)}))
            if 0 <= time - 6 < len(lane):
                c = lane[time - 6]
                out, turn = place(
                    turn, c["theirs_sent"], c["theirs"], out, c["base"], (tokens, columns)
                )
        for lane in lanes:
            if time < len(lane):
                turn = run(turn, [leave_of(lane[time])])
        some = chunks[2 * time + 2 : 2 * time + 4]
        if some:
            turn = project_some(turn, some)
    return out


def solution(mesh):
    in_specs = (
        P("groups", "tensor"),
        P(("groups", "tensor"), None),
        P(("groups", "tensor"), None),
        P(("groups", "tensor")),
        P("groups"),
        P("tensor", None),
    )
    out_specs = P("groups", None)
    return jax.shard_map(
        functools.partial(shards, mesh.shape["tensor"]),
        mesh=mesh,
        in_specs=in_specs,
        out_specs=out_specs,
        check_vma=False,
    )
```

time: 180 us -> 167 us (0.928)
  waiting for transfers between devices: 21.8 us -> 34.1 us
  Pallas kernels: 53.1 us -> 42.9 us
  starting transfers between devices: 93.4 us -> 85.9 us
  between operations: 7.13 us -> 1.97 us
  local copies, waits for them, and re-layouts: 3.71 us -> 1.91 us
    ppermute x59 -> x60, waiting for transfers between devices: 21.8 us -> 34.1 us  [swap(): return lax.ppermute(x, 'tensor', [(d, d ^ bits) for d in range(devices)])]
    ppermute x59 -> x60, starting transfers between devices: 88.1 us -> 80.6 us  [swap(): return lax.ppermute(x, 'tensor', [(d, d ^ bits) for d in range(devices)])]
    pallas_call x2 -> x1, Pallas kernels: 9.55 us -> 2.46 us  [pack(): pl.pallas_call(functools.partial(pack_kernel, local_heads), out_shape=[ja...]
    pallas_call x28 -> x39, Pallas kernels: 43.6 us -> 40.5 us  [call(): pl.pallas_call(in_order(kernel, len(args), len(out_shapes)), out_shape=[*...]
  transfers between devices with their start and end apart: 67 -> 68, of which waited for: 18 -> 19; matrix products, arithmetic and copies ran while one was open for 0% -> 0% of each run, Pallas kernels for 13% -> 17%
where the time goes in v2:
time: 167 us
  starting transfers between devices  85.9 us (51%)
  Pallas kernels  42.9 us (26%)
  waiting for transfers between devices  34.1 us (20%)
  between operations  1.97 us (1%)
  local copies, waits for them, and re-layouts  1.91 us (1%)
    ppermute x60, starting transfers between devices, swap(): return lax.ppermute(x, 'tensor', [(d, d ^ bits) for d in range(devices)])  80.6 us
    pallas_call x39, Pallas kernels, call(): pl.pallas_call(in_order(kernel, len(args), len(out_shapes)), out_shape=[*...  40.5 us
    ppermute x60, waiting for transfers between devices, swap(): return lax.ppermute(x, 'tensor', [(d, d ^ bits) for d in range(devices)])  34.1 us
    ppermute x8, starting transfers between devices, along(): return lax.ppermute(x, 'tensor', perm)  5.33 us
  transfers between devices with their start and end apart: 68, of which 19 were waited for; matrix products, arithmetic and copies ran while one was open for 0% of the time, Pallas kernels for 17%

profile of v2, /device:TPU:1, one launch (start us, length us, event | category | flops | bytes accessed | tf_op | source)
XLA Modules:
  0.0 166.9 jit_solution(13589816467498547021)
XLA Ops:
  0.7 2.5 %pack_kv.1 = (bf16[256,1024]{1,0:T(8,128)(2,1)}, bf16[272,128]{1,0:T(8,128)(2,1)}, bf16[272,128]{1,0:T(8,128)(2,1)}, bf16[272,128]{1,0:T(8,128)(2,1)}, bf16[272,...) custom-call(s32[1]{0:T(128)S(6)} %copy.21.lengths_ref, ...), custom_call_target="tpu_custom_call" | custom-call | tf_op jit(solution)/shard_map/pack_kv/pallas_call | solution.py:57
  6.6 2.4 %collective-permute-start.3 = (bf16[272,128]{1,0:T(8,128)(2,1)}, bf16[272,128]{1,0:T(8,128)(2,1)S(1)}, u32[]{:S(2)}, u32[]{:S(2)}) collective-permute-start(bf16[272,128]{1,0:T(8,128)(2,1)} %get-tuple-element.146), channel_id=1, source_target_pairs={{0,8},{1,9},{2,10},{3,11},{4,12},{5,13},{6,14},{7,15},{8,0},{9,1},... | collective-permute-start | bytes 208904 | tf_op jit(solution)/shard_map/ppermute | solution.py:381
  10.0 3.3 %collective-permute-start.5 = (bf16[272,128]{1,0:T(8,128)(2,1)}, bf16[272,128]{1,0:T(8,128)(2,1)S(1)}, u32[]{:S(2)}, u32[]{:S(2)}) collective-permute-start(bf16[272,128]{1,0:T(8,128)(2,1)} %get-tuple-element.148), channel_id=1, source_target_pairs={{0,12},{1,13},{2,14},{3,15},{4,8},{5,9},{6,10},{7,11},{8,4},{9,5},... | collective-permute-start | bytes 208904 | tf_op jit(solution)/shard_map/ppermute | solution.py:381
  13.3 6.5 %collective-permute-done.4.refs_5_ = bf16[272,128]{1,0:T(8,128)(2,1)S(1)} collective-permute-done((bf16[272,128]{1,0:T(8,128)(2,1)}, bf16[272,128]{1,0:T(8,128)(2,1)S(1)}, u32[]{:S(2)}, u32[]{:S(2)}) %collective-permute-start.4) | collective-permute-done | bytes 69664 | tf_op jit(solution)/shard_map/ppermute | solution.py:381
  20.8 3.2 %collective-permute-start.7 = (bf16[8,272,128]{2,1,0:T(8,128)(2,1)S(1)}, bf16[8,272,128]{2,1,0:T(8,128)(2,1)S(1)}, u32[]{:S(2)}, u32[]{:S(2)}) collective-permute-start(bf16[8,272,128]{2,1,0:T(8,128)(2,1)S(1)} %get-tuple-element.150.refs_2_), channel_id=1, source_target_pairs={{0,1},{1,0},{2,3},{3,2},{4,5},{5,4},{6,7},{7,6},{8,9},{9,8},{10,11... | collective-permute-start | bytes 1671176 | tf_op jit(solution)/shard_map/ppermute | solution.py:381
  25.7 4.1 %attention_mine.1 = (f32[256,1024]{1,0:T(8,128)S(1)}, f32[256,8]{1,0:T(8,128)S(1)}, f32[256,8]{1,0:T(8,128)S(1)}, f32[8,128]{1,0:T(8,128)S(1)}) custom-call(s32[1]{0:T(128)S(6)} %copy.22.refs_0_, bf16[256,1024]{1,0:T(8,128)(2,1)S(1)} %copy-done, bf16[8,272,128]{2,1,0:T(8,128)(2,1)S(1)} %get-tuple-element.150.refs_2_, f32[8,128]{1,0:T(8,128)S(1)} %get-tuple-element.151.refs_3_), custom_call_target="tpu_custom_call" | custom-call | bytes 16777216 | tf_op jit(solution)/shard_map/attention_mine/pallas_call | solution.py:192
  29.8 5.4 %attention_theirs.1 = (bf16[256,1024]{1,0:T(8,128)(2,1)S(1)}, f32[8,128]{1,0:T(8,128)S(1)}) custom-call(s32[1]{0:T(128)S(6)} %copy.22.refs_0_, bf16[256,1024]{1,0:T(8,128)(2,1)S(1)} %copy-done, bf16[8,272,128]{2,1,0:T(8,128)(2,1)S(1)} %collective-permute-done.7.refs_2_, f32[256,1024]{1,0:T(8,128)S(1)} %get-tuple-element.152.refs_3_, ...), custom_call_target="tpu_custom_call" | custom-call | bytes 16777216 | tf_op jit(solution)/shard_map/attention_theirs/pallas_call | solution.py:192
  35.2 4.8 %project.4 = (bf16[128,1024]{1,0:T(8,128)(2,1)S(1)}, bf16[128,1024]{1,0:T(8,128)(2,1)S(1)}, bf16[128,1024]{1,0:T(8,128)(2,1)S(1)}, bf16[128,1024]{1,0:T(8,128)(2...) custom-call(bf16[256,1024]{1,0:T(8,128)(2,1)S(1)} %get-tuple-element, ...), custom_call_target="tpu_custom_call" | custom-call | bytes 131072 | tf_op jit(solution)/shard_map/project/pallas_call | solution.py:192
  43.8 5.0 %project.5 = (bf16[128,1024]{1,0:T(8,128)(2,1)S(1)}, bf16[128,1024]{1,0:T(8,128)(2,1)S(1)}, bf16[128,1024]{1,0:T(8,128)(2,1)S(1)}, bf16[128,1024]{1,0:T(8,128)(2...) custom-call(bf16[256,1024]{1,0:T(8,128)(2,1)S(1)} %get-tuple-element, ...), custom_call_target="tpu_custom_call" | custom-call | bytes 131072 | tf_op jit(solution)/shard_map/project/pallas_call | solution.py:192
  51.1 4.0 %collective-permute-done.13.refs_2_.refs_5_ = bf16[128,1024]{1,0:T(8,128)(2,1)S(1)} collective-permute-done((bf16[128,1024]{1,0:T(8,128)(2,1)S(1)}, bf16[128,1024]{1,0:T(8,128)(2,1)S(1)}, u32[]{:S(2)}, u32[]{:S(2)}) %collective-permute-start.13) | collective-permute-done | bytes 262176 | tf_op jit(solution)/shard_map/ppermute | solution.py:381
  60.3 4.8 %project.6 = (bf16[128,1024]{1,0:T(8,128)(2,1)S(1)}, bf16[128,1024]{1,0:T(8,128)(2,1)S(1)}, bf16[128,1024]{1,0:T(8,128)(2,1)S(1)}, bf16[128,1024]{1,0:T(8,128)(2...) custom-call(bf16[256,1024]{1,0:T(8,128)(2,1)S(1)} %get-tuple-element, ...), custom_call_target="tpu_custom_call" | custom-call | bytes 131072 | tf_op jit(solution)/shard_map/project/pallas_call | solution.py:192
  67.8 3.6 %collective-permute-done.21.refs_6_ = bf16[128,1024]{1,0:T(8,128)(2,1)S(1)} collective-permute-done((bf16[128,1024]{1,0:T(8,128)(2,1)S(1)}, bf16[128,1024]{1,0:T(8,128)(2,1)S(1)}, u32[]{:S(2)}, u32[]{:S(2)}) %collective-permute-start.21) | collective-permute-done | bytes 262176 | tf_op jit(solution)/shard_map/ppermute | solution.py:381
  73.5 3.9 %collective-permute-start.31 = (bf16[128,1024]{1,0:T(8,128)(2,1)S(1)}, bf16[128,1024]{1,0:T(8,128)(2,1)S(1)}, u32[]{:S(2)}, u32[]{:S(2)}) collective-permute-start(bf16[128,1024]{1,0:T(8,128)(2,1)S(1)} %get-tuple-element.205), channel_id=1, source_target_pairs={{0,4},{1,5},{2,6},{3,7},{4,0},{5,1},{6,2},{7,3},{8,12},{9,13},{10,... | collective-permute-start | bytes 786440 | tf_op jit(solution)/shard_map/ppermute | solution.py:381
  80.1 3.1 %collective-permute-start.27 = (bf16[128,1024]{1,0:T(8,128)(2,1)S(1)}, bf16[128,1024]{1,0:T(8,128)(2,1)S(1)}, u32[]{:S(2)}, u32[]{:S(2)}) collective-permute-start(bf16[128,1024]{1,0:T(8,128)(2,1)S(1)} %get-tuple-element.200), channel_id=1, source_target_pairs={{0,4},{1,5},{2,6},{3,7},{4,0},{5,1},{6,2},{7,3},{8,12},{9,13},{10,... | collective-permute-start | bytes 786440 | tf_op jit(solution)/shard_map/ppermute | solution.py:381
  83.2 4.8 %project.7 = (bf16[128,1024]{1,0:T(8,128)(2,1)S(1)}, bf16[128,1024]{1,0:T(8,128)(2,1)S(1)}, bf16[128,1024]{1,0:T(8,128)(2,1)S(1)}, bf16[128,1024]{1,0:T(8,128)(2...) custom-call(bf16[256,1024]{1,0:T(8,128)(2,1)S(1)} %get-tuple-element, ...), custom_call_target="tpu_custom_call" | custom-call | bytes 131072 | tf_op jit(solution)/shard_map/project/pallas_call | solution.py:192
  88.0 3.0 %collective-permute-start.35 = (bf16[128,1024]{1,0:T(8,128)(2,1)S(1)}, bf16[128,1024]{1,0:T(8,128)(2,1)S(1)}, u32[]{:S(2)}, u32[]{:S(2)}) collective-permute-start(bf16[128,1024]{1,0:T(8,128)(2,1)S(1)} %get-tuple-element.215), channel_id=1, source_target_pairs={{0,1},{1,0},{2,3},{3,2},{4,5},{5,4},{6,7},{7,6},{8,9},{9,8},{10,11... | collective-permute-start | bytes 786440 | tf_op jit(solution)/shard_map/ppermute | solution.py:381
  95.8 4.7 %collective-permute-done.40.refs_4_.refs_6_ = bf16[128,1024]{1,0:T(8,128)(2,1)S(1)} collective-permute-done((bf16[128,1024]{1,0:T(8,128)(2,1)S(1)}, bf16[128,1024]{1,0:T(8,128)(2,1)S(1)}, u32[]{:S(2)}, u32[]{:S(2)}) %collective-permute-start.40) | collective-permute-done | bytes 262176 | tf_op jit(solution)/shard_map/ppermute | solution.py:381
  107.5 2.8 %collective-permute-start.42 = (bf16[128,1024]{1,0:T(8,128)(2,1)S(1)}, bf16[128,1024]{1,0:T(8,128)(2,1)S(1)}, u32[]{:S(2)}, u32[]{:S(2)}) collective-permute-start(bf16[128,1024]{1,0:T(8,128)(2,1)S(1)} %get-tuple-element.227.refs_1_), channel_id=1, source_target_pairs={{0,4},{1,5},{2,6},{3,7},{4,0},{5,1},{6,2},{7,3},{8,12},{9,13},{10,... | collective-permute-start | bytes 786440 | tf_op jit(solution)/shard_map/ppermute | solution.py:381
  113.3 2.6 %collective-permute-start.52 = (bf16[128,1024]{1,0:T(8,128)(2,1)S(1)}, bf16[128,1024]{1,0:T(8,128)(2,1)S(1)}, u32[]{:S(2)}, u32[]{:S(2)}) collective-permute-start(bf16[128,1024]{1,0:T(8,128)(2,1)S(1)} %get-tuple-element.239.refs_1_), channel_id=1, source_target_pairs={{0,4},{1,5},{2,6},{3,7},{4,0},{5,1},{6,2},{7,3},{8,12},{9,13},{10,... | collective-permute-start | bytes 786440 | tf_op jit(solution)/shard_map/ppermute | solution.py:381
  118.0 4.5 %collective-permute-start.51 = (bf16[2,128,1024]{2,1,0:T(8,128)(2,1)S(1)}, bf16[2,128,1024]{2,1,0:T(8,128)(2,1)S(1)}, u32[]{:S(2)}, u32[]{:S(2)}) collective-permute-start(bf16[2,128,1024]{2,1,0:T(8,128)(2,1)S(1)} %get-tuple-element.238.refs_0_), channel_id=1, source_target_pairs={{0,1},{1,0},{2,3},{3,2},{4,5},{5,4},{6,7},{7,6},{8,9},{9,8},{10,11... | collective-permute-start | bytes 1572872 | tf_op jit(solution)/shard_map/ppermute | solution.py:381
  124.9 3.5 %collective-permute-start.48 = (bf16[128,1024]{1,0:T(8,128)(2,1)S(1)}, bf16[128,1024]{1,0:T(8,128)(2,1)S(1)}, u32[]{:S(2)}, u32[]{:S(2)}) collective-permute-start(bf16[128,1024]{1,0:T(8,128)(2,1)S(1)} %get-tuple-element.235.refs_1_), channel_id=1, source_target_pairs={{0,4},{1,5},{2,6},{3,7},{4,0},{5,1},{6,2},{7,3},{8,12},{9,13},{10,... | collective-permute-start | bytes 786440 | tf_op jit(solution)/shard_map/ppermute | solution.py:381
  132.3 2.6 %collective-permute-done.48.refs_0_ = bf16[128,1024]{1,0:T(8,128)(2,1)S(1)} collective-permute-done((bf16[128,1024]{1,0:T(8,128)(2,1)S(1)}, bf16[128,1024]{1,0:T(8,128)(2,1)S(1)}, u32[]{:S(2)}, u32[]{:S(2)}) %collective-permute-start.48) | collective-permute-done | bytes 262176 | tf_op jit(solution)/shard_map/ppermute | solution.py:381
  150.4 3.8 %collective-permute-start.67 = (bf16[2,128,1024]{2,1,0:T(8,128)(2,1)S(1)}, bf16[2,128,1024]{2,1,0:T(8,128)(2,1)S(1)}, u32[]{:S(2)}, u32[]{:S(2)}) collective-permute-start(bf16[2,128,1024]{2,1,0:T(8,128)(2,1)S(1)} %get-tuple-element.269.refs_0_), channel_id=1, source_target_pairs={{0,1},{1,0},{2,3},{3,2},{4,5},{5,4},{6,7},{7,6},{8,9},{9,8},{10,11... | collective-permute-start | bytes 1572872 | tf_op jit(solution)/shard_map/ppermute | solution.py:381
  155.2 4.1 %collective-permute-start.66 = (bf16[2,128,1024]{2,1,0:T(8,128)(2,1)S(1)}, bf16[2,128,1024]{2,1,0:T(8,128)(2,1)S(1)}, u32[]{:S(2)}, u32[]{:S(2)}) collective-permute-start(bf16[2,128,1024]{2,1,0:T(8,128)(2,1)S(1)} %get-tuple-element.268.refs_0_), channel_id=1, source_target_pairs={{0,1},{1,0},{2,3},{3,2},{4,5},{5,4},{6,7},{7,6},{8,9},{9,8},{10,11... | collective-permute-start | bytes 1572872 | tf_op jit(solution)/shard_map/ppermute | solution.py:381
  (157 shorter events, 72.0 us)
Async XLA Ops:
  9.0 10.9 %collective-permute-start.4 = (bf16[272,128]{1,0:T(8,128)(2,1)}, bf16[272,128]{1,0:T(8,128)(2,1)S(1)}, u32[]{:S(2)}, u32[]{:S(2)}) collective-permute-start(bf16[272,128]{1,0:T(8,128)(2,1)} %get-tuple-element.147), channel_id=1, source_target_pairs={{0,10},{1,11},{2,8},{3,9},{4,14},{5,15},{6,12},{7,13},{8,2},{9,3},... | collective-permute-start | bytes 208904 | tf_op jit(solution)/shard_map/ppermute | solution.py:381
  42.5 12.7 %collective-permute-start.13 = (bf16[128,1024]{1,0:T(8,128)(2,1)S(1)}, bf16[128,1024]{1,0:T(8,128)(2,1)S(1)}, u32[]{:S(2)}, u32[]{:S(2)}) collective-permute-start(bf16[128,1024]{1,0:T(8,128)(2,1)S(1)} %get-tuple-element.171), channel_id=1, source_target_pairs={{0,2},{1,3},{2,0},{3,1},{4,6},{5,7},{6,4},{7,5},{8,10},{9,11},{10,... | collective-permute-start | bytes 786440 | tf_op jit(solution)/shard_map/ppermute | solution.py:381
  49.5 10.7 %collective-permute-start.22 = (bf16[128,1024]{1,0:T(8,128)(2,1)S(1)}, bf16[128,1024]{1,0:T(8,128)(2,1)S(1)}, u32[]{:S(2)}, u32[]{:S(2)}) collective-permute-start(bf16[128,1024]{1,0:T(8,128)(2,1)S(1)} %get-tuple-element.191), channel_id=1, source_target_pairs={{0,1},{1,0},{2,3},{3,2},{4,5},{5,4},{6,7},{7,6},{8,9},{9,8},{10,11... | collective-permute-start | bytes 786440 | tf_op jit(solution)/shard_map/ppermute | solution.py:381
  55.6 11.2 %collective-permute-start.19 = (bf16[128,1024]{1,0:T(8,128)(2,1)S(1)}, bf16[128,1024]{1,0:T(8,128)(2,1)S(1)}, u32[]{:S(2)}, u32[]{:S(2)}) collective-permute-start(bf16[128,1024]{1,0:T(8,128)(2,1)S(1)} %get-tuple-element.187), channel_id=1, source_target_pairs={{0,1},{1,0},{2,3},{3,2},{4,5},{5,4},{6,7},{7,6},{8,9},{9,8},{10,11... | collective-permute-start | bytes 786440 | tf_op jit(solution)/shard_map/ppermute | solution.py:381
  60.2 11.2 %collective-permute-start.21 = (bf16[128,1024]{1,0:T(8,128)(2,1)S(1)}, bf16[128,1024]{1,0:T(8,128)(2,1)S(1)}, u32[]{:S(2)}, u32[]{:S(2)}) collective-permute-start(bf16[128,1024]{1,0:T(8,128)(2,1)S(1)} %get-tuple-element.189), channel_id=1, source_target_pairs={{0,4},{1,5},{2,6},{3,7},{4,0},{5,1},{6,2},{7,3},{8,12},{9,13},{10,... | collective-permute-start | bytes 786440 | tf_op jit(solution)/shard_map/ppermute | solution.py:381
  65.8 11.6 %collective-permute-start.17 = (bf16[128,1024]{1,0:T(8,128)(2,1)S(1)}, bf16[128,1024]{1,0:T(8,128)(2,1)S(1)}, u32[]{:S(2)}, u32[]{:S(2)}) collective-permute-start(bf16[128,1024]{1,0:T(8,128)(2,1)S(1)} %get-tuple-element.183), channel_id=1, source_target_pairs={{0,1},{1,0},{2,3},{3,2},{4,5},{5,4},{6,7},{7,6},{8,9},{9,8},{10,11... | collective-permute-start | bytes 786440 | tf_op jit(solution)/shard_map/ppermute | solution.py:381
  66.8 12.3 %collective-permute-start.28 = (bf16[128,1024]{1,0:T(8,128)(2,1)S(1)}, bf16[128,1024]{1,0:T(8,128)(2,1)S(1)}, u32[]{:S(2)}, u32[]{:S(2)}) collective-permute-start(bf16[128,1024]{1,0:T(8,128)(2,1)S(1)} %get-tuple-element.202), channel_id=1, source_target_pairs={{0,1},{1,0},{2,3},{3,2},{4,5},{5,4},{6,7},{7,6},{8,9},{9,8},{10,11... | collective-permute-start | bytes 786440 | tf_op jit(solution)/shard_map/ppermute | solution.py:381
  73.5 14.6 %collective-permute-start.31 = (bf16[128,1024]{1,0:T(8,128)(2,1)S(1)}, bf16[128,1024]{1,0:T(8,128)(2,1)S(1)}, u32[]{:S(2)}, u32[]{:S(2)}) collective-permute-start(bf16[128,1024]{1,0:T(8,128)(2,1)S(1)} %get-tuple-element.205), channel_id=1, source_target_pairs={{0,4},{1,5},{2,6},{3,7},{4,0},{5,1},{6,2},{7,3},{8,12},{9,13},{10,... | collective-permute-start | bytes 786440 | tf_op jit(solution)/shard_map/ppermute | solution.py:381
  77.4 13.8 %collective-permute-start.16 = (bf16[128,1024]{1,0:T(8,128)(2,1)S(1)}, bf16[128,1024]{1,0:T(8,128)(2,1)S(1)}, u32[]{:S(2)}, u32[]{:S(2)}) collective-permute-start(bf16[128,1024]{1,0:T(8,128)(2,1)S(1)} %get-tuple-element.181), channel_id=1, source_target_pairs={{0,1},{1,0},{2,3},{3,2},{4,5},{5,4},{6,7},{7,6},{8,9},{9,8},{10,11... | collective-permute-start | bytes 786440 | tf_op jit(solution)/shard_map/ppermute | solution.py:381
  79.1 12.2 %collective-permute-start.25 = (bf16[128,1024]{1,0:T(8,128)(2,1)S(1)}, bf16[128,1024]{1,0:T(8,128)(2,1)S(1)}, u32[]{:S(2)}, u32[]{:S(2)}) collective-permute-start(bf16[128,1024]{1,0:T(8,128)(2,1)S(1)} %get-tuple-element.198), channel_id=1, source_target_pairs={{0,2},{1,3},{2,0},{3,1},{4,6},{5,7},{6,4},{7,5},{8,10},{9,11},{10,... | collective-permute-start | bytes 786440 | tf_op jit(solution)/shard_map/ppermute | solution.py:381
  79.4 12.4 %collective-permute-start.26 = (bf16[128,1024]{1,0:T(8,128)(2,1)S(1)}, bf16[128,1024]{1,0:T(8,128)(2,1)S(1)}, u32[]{:S(2)}, u32[]{:S(2)}) collective-permute-start(bf16[128,1024]{1,0:T(8,128)(2,1)S(1)} %get-tuple-element.199.refs_3_), channel_id=1, source_target_pairs={{4,8},{5,9},{6,10},{7,11},{8,4},{9,5},{10,6},{11,7},{20,24},{21,25... | collective-permute-start | bytes 786440 | tf_op jit(solution)/shard_map/ppermute | solution.py:385
  80.1 11.7 %collective-permute-start.27 = (bf16[128,1024]{1,0:T(8,128)(2,1)S(1)}, bf16[128,1024]{1,0:T(8,128)(2,1)S(1)}, u32[]{:S(2)}, u32[]{:S(2)}) collective-permute-start(bf16[128,1024]{1,0:T(8,128)(2,1)S(1)} %get-tuple-element.200), channel_id=1, source_target_pairs={{0,4},{1,5},{2,6},{3,7},{4,0},{5,1},{6,2},{7,3},{8,12},{9,13},{10,... | collective-permute-start | bytes 786440 | tf_op jit(solution)/shard_map/ppermute | solution.py:381
  107.5 10.5 %collective-permute-start.42 = (bf16[128,1024]{1,0:T(8,128)(2,1)S(1)}, bf16[128,1024]{1,0:T(8,128)(2,1)S(1)}, u32[]{:S(2)}, u32[]{:S(2)}) collective-permute-start(bf16[128,1024]{1,0:T(8,128)(2,1)S(1)} %get-tuple-element.227.refs_1_), channel_id=1, source_target_pairs={{0,4},{1,5},{2,6},{3,7},{4,0},{5,1},{6,2},{7,3},{8,12},{9,13},{10,... | collective-permute-start | bytes 786440 | tf_op jit(solution)/shard_map/ppermute | solution.py:381
  110.3 12.2 %collective-permute-start.43 = (bf16[128,1024]{1,0:T(8,128)(2,1)S(1)}, bf16[128,1024]{1,0:T(8,128)(2,1)S(1)}, u32[]{:S(2)}, u32[]{:S(2)}) collective-permute-start(bf16[128,1024]{1,0:T(8,128)(2,1)S(1)} %get-tuple-element.228.refs_2_), channel_id=1, source_target_pairs={{4,8},{5,9},{6,10},{7,11},{8,4},{9,5},{10,6},{11,7},{20,24},{21,25... | collective-permute-start | bytes 786440 | tf_op jit(solution)/shard_map/ppermute | solution.py:385
  112.5 11.8 %collective-permute-start.44 = (bf16[128,1024]{1,0:T(8,128)(2,1)S(1)}, bf16[128,1024]{1,0:T(8,128)(2,1)S(1)}, u32[]{:S(2)}, u32[]{:S(2)}) collective-permute-start(bf16[128,1024]{1,0:T(8,128)(2,1)S(1)} %get-tuple-element.229.refs_8_), channel_id=1, source_target_pairs={{0,2},{1,3},{2,0},{3,1},{4,6},{5,7},{6,4},{7,5},{8,10},{9,11},{10,... | collective-permute-start | bytes 786440 | tf_op jit(solution)/shard_map/ppermute | solution.py:381
  113.3 11.6 %collective-permute-start.52 = (bf16[128,1024]{1,0:T(8,128)(2,1)S(1)}, bf16[128,1024]{1,0:T(8,128)(2,1)S(1)}, u32[]{:S(2)}, u32[]{:S(2)}) collective-permute-start(bf16[128,1024]{1,0:T(8,128)(2,1)S(1)} %get-tuple-element.239.refs_1_), channel_id=1, source_target_pairs={{0,4},{1,5},{2,6},{3,7},{4,0},{5,1},{6,2},{7,3},{8,12},{9,13},{10,... | collective-permute-start | bytes 786440 | tf_op jit(solution)/shard_map/ppermute | solution.py:381
  115.9 12.4 %collective-permute-start.53 = (bf16[128,1024]{1,0:T(8,128)(2,1)S(1)}, bf16[128,1024]{1,0:T(8,128)(2,1)S(1)}, u32[]{:S(2)}, u32[]{:S(2)}) collective-permute-start(bf16[128,1024]{1,0:T(8,128)(2,1)S(1)} %get-tuple-element.240.refs_2_), channel_id=1, source_target_pairs={{4,8},{5,9},{6,10},{7,11},{8,4},{9,5},{10,6},{11,7},{20,24},{21,25... | collective-permute-start | bytes 786440 | tf_op jit(solution)/shard_map/ppermute | solution.py:385
  118.0 19.4 %collective-permute-start.51 = (bf16[2,128,1024]{2,1,0:T(8,128)(2,1)S(1)}, bf16[2,128,1024]{2,1,0:T(8,128)(2,1)S(1)}, u32[]{:S(2)}, u32[]{:S(2)}) collective-permute-start(bf16[2,128,1024]{2,1,0:T(8,128)(2,1)S(1)} %get-tuple-element.238.refs_0_), channel_id=1, source_target_pairs={{0,1},{1,0},{2,3},{3,2},{4,5},{5,4},{6,7},{7,6},{8,9},{9,8},{10,11... | collective-permute-start | bytes 1572872 | tf_op jit(solution)/shard_map/ppermute | solution.py:381
  124.5 15.6 %collective-permute-start.58 = (bf16[2,128,1024]{2,1,0:T(8,128)(2,1)S(1)}, bf16[2,128,1024]{2,1,0:T(8,128)(2,1)S(1)}, u32[]{:S(2)}, u32[]{:S(2)}) collective-permute-start(bf16[2,128,1024]{2,1,0:T(8,128)(2,1)S(1)} %get-tuple-element.248.refs_0_), channel_id=1, source_target_pairs={{0,1},{1,0},{2,3},{3,2},{4,5},{5,4},{6,7},{7,6},{8,9},{9,8},{10,11... | collective-permute-start | bytes 1572872 | tf_op jit(solution)/shard_map/ppermute | solution.py:381
  136.2 10.5 %collective-permute-start.57 = (bf16[2,128,1024]{2,1,0:T(8,128)(2,1)S(1)}, bf16[2,128,1024]{2,1,0:T(8,128)(2,1)S(1)}, u32[]{:S(2)}, u32[]{:S(2)}) collective-permute-start(bf16[2,128,1024]{2,1,0:T(8,128)(2,1)S(1)} %get-tuple-element.247.refs_0_), channel_id=1, source_target_pairs={{0,1},{1,0},{2,3},{3,2},{4,5},{5,4},{6,7},{7,6},{8,9},{9,8},{10,11... | collective-permute-start | bytes 1572872 | tf_op jit(solution)/shard_map/ppermute | solution.py:381
  140.2 14.0 %collective-permute-start.63 = (bf16[2,128,1024]{2,1,0:T(8,128)(2,1)S(1)}, bf16[2,128,1024]{2,1,0:T(8,128)(2,1)S(1)}, u32[]{:S(2)}, u32[]{:S(2)}) collective-permute-start(bf16[2,128,1024]{2,1,0:T(8,128)(2,1)S(1)} %get-tuple-element.259.refs_0_), channel_id=1, source_target_pairs={{0,1},{1,0},{2,3},{3,2},{4,5},{5,4},{6,7},{7,6},{8,9},{9,8},{10,11... | collective-permute-start | bytes 1572872 | tf_op jit(solution)/shard_map/ppermute | solution.py:381
  145.3 14.0 %collective-permute-start.62 = (bf16[2,128,1024]{2,1,0:T(8,128)(2,1)S(1)}, bf16[2,128,1024]{2,1,0:T(8,128)(2,1)S(1)}, u32[]{:S(2)}, u32[]{:S(2)}) collective-permute-start(bf16[2,128,1024]{2,1,0:T(8,128)(2,1)S(1)} %get-tuple-element.258.refs_0_), channel_id=1, source_target_pairs={{0,1},{1,0},{2,3},{3,2},{4,5},{5,4},{6,7},{7,6},{8,9},{9,8},{10,11... | collective-permute-start | bytes 1572872 | tf_op jit(solution)/shard_map/ppermute | solution.py:381
  149.0 11.7 %collective-permute-start.61 = (bf16[128,1024]{1,0:T(8,128)(2,1)S(1)}, bf16[128,1024]{1,0:T(8,128)(2,1)S(1)}, u32[]{:S(2)}, u32[]{:S(2)}) collective-permute-start(bf16[128,1024]{1,0:T(8,128)(2,1)S(1)} %get-tuple-element.257.refs_0_), channel_id=1, source_target_pairs={{0,2},{1,3},{2,0},{3,1},{4,6},{5,7},{6,4},{7,5},{8,10},{9,11},{10,... | collective-permute-start | bytes 786440 | tf_op jit(solution)/shard_map/ppermute | solution.py:381
  150.4 12.7 %collective-permute-start.67 = (bf16[2,128,1024]{2,1,0:T(8,128)(2,1)S(1)}, bf16[2,128,1024]{2,1,0:T(8,128)(2,1)S(1)}, u32[]{:S(2)}, u32[]{:S(2)}) collective-permute-start(bf16[2,128,1024]{2,1,0:T(8,128)(2,1)S(1)} %get-tuple-element.269.refs_0_), channel_id=1, source_target_pairs={{0,1},{1,0},{2,3},{3,2},{4,5},{5,4},{6,7},{7,6},{8,9},{9,8},{10,11... | collective-permute-start | bytes 1572872 | tf_op jit(solution)/shard_map/ppermute | solution.py:381
  (46 other events, 331.3 us)

commit v3 on v2

--- a/solution.py
+++ b/solution.py
@@ -14,11 +14,12 @@
 GROUP = HEADS // KV_HEADS
 FLAG_ROWS = 16
 CHUNKS = 8
-BLOCK_COLS = 512
-SLOTS = 8
+BLOCK_COLS = 1024
+SLOTS = 4
+STEP_FLOPS = 3 * 10**9
 VMEM_LIMIT = 32 * 1024 * 1024
 PACK_VMEM_LIMIT = 56 * 1024 * 1024
-ATTENTION_ROWS = 256
+A3000000000ENTION_ROWS = 256
 
 
 def position():
@@ -98,19 +99,20 @@
     token = lax.broadcasted_iota(jnp.int32, (tokens, slots), 0) + start_ref[0]
     lane = lax.broadcasted_iota(jnp.int32, (tokens, slots), 1)
     lane_row = lax.broadcasted_iota(jnp.int32, (1, slots), 1).astype(jnp.float32)
-    for m in range(pieces.shape[0]):
-        rows = slice(m * slots, (m + 1) * slots)
-        keys[rows, :] = pieces[m, :slots, :]
-        values[rows, :] = pieces[m, slots : 2 * slots, :]
-        length = pieces[m, 2 * slots :, :].astype(jnp.float32)[:1, :slots]
+    for i in range(pieces.shape[0]):
+        m = pieces.shape[0] - 1 - i
+        rows = slice(i * slots, (i + 1) * slots)
+        keys[rows, :] = pieces[i, :slots, :]
+        values[rows, :] = pieces[i, slots : 2 * slots, :]
+        length = pieces[i, 2 * slots :, :].astype(jnp.float32)[:1, :slots]
         dead = jnp.where(lane_row < length, 0.0, -1e30)
         shard = (chip ^ m) * 2 + (core ^ flip)
         bias[:, rows] = jnp.where(lane + shard * slots <= token, dead, -1e30)
     factor = HEAD_DIM ** (-0.5) * math.log2(math.e)
     for head in range(queries.shape[1] // HEAD_DIM):
         cols = slice(head * HEAD_DIM, (head + 1) * HEAD_DIM)
-        for block in range(tokens // ATTENTION_ROWS):
-            rows = slice(block * ATTENTION_ROWS, (block + 1) * ATTENTION_ROWS)
+        for block in range(tokens // A3000000000ENTION_ROWS):
+            rows = slice(block * A3000000000ENTION_ROWS, (block + 1) * A3000000000ENTION_ROWS)
             scores = lax.dot_general(
                 queries[rows, cols],
                 keys[...],
@@ -132,11 +134,11 @@
                 total = total + near_total[rows, head : head + 1] * shrink
                 mixed = mixed + near[rows, cols] * shrink
                 result = (mixed / total).astype(jnp.bfloat16)
-                for i in range(0, ATTENTION_ROWS, min(half, ATTENTION_ROWS)):
-                    first = block * ATTENTION_ROWS + i
+                for i in range(0, A3000000000ENTION_ROWS, min(half, A3000000000ENTION_ROWS)):
+                    first = block * A3000000000ENTION_ROWS + i
                     first = first + core * jnp.where(first < half, half, -half)
-                    place = pl.ds(pl.multiple_of(first, 128), min(half, ATTENTION_ROWS))
-                    out_ref[place, cols] = result[i : i + min(half, ATTENTION_ROWS)]
+                    place = pl.ds(pl.multiple_of(first, 128), min(half, A3000000000ENTION_ROWS))
+                    out_ref[place, cols] = result[i : i + min(half, A3000000000ENTION_ROWS)]
             else:
                 near[rows, cols] = mixed
                 near_top[rows, head : head + 1] = top
@@ -197,7 +199,7 @@
         scratch_shapes=list(scratch),
         input_output_aliases=aliases or {},
         compiler_params=pltpu.CompilerParams(vmem_limit_bytes=VMEM_LIMIT),
-        cost_estimate=pl.CostEstimate(flops=0, bytes_accessed=bytes_accessed, transcendentals=0),
+        cost_estimate=pl.CostEstimate(flops=STEP_FLOPS, bytes_accessed=bytes_accessed, transcendentals=0),
         name=name,
     )(*args, turn)
     return results, turn
@@ -387,7 +389,7 @@
     turn = jnp.zeros((8, 128), jnp.float32)
     fetched, *packed = pack(chips, local_heads, lengths, queries, keys, values)
     direct = {m: swap(packed[m], 2 * m) if m else packed[0] for m in reversed(range(chips))}
-    mine, turn = bundle(turn, [direct[m] for m in range(chips)])
+    mine, turn = bundle(turn, [direct[m] for m in reversed(range(chips))])
     theirs = swap(mine, 1)
     sums, turn = attention(turn, start_pos, fetched, mine, 0)
     (attended,), turn = attention(turn, start_pos, fetched, theirs, 1, sums)
@@ -449,7 +451,11 @@
         return turn
 
     lanes = [chunks[0::2], chunks[1::2]]
-    turn = project_some(turn, chunks[:2])
+    turn = project_some(turn, chunks[:1])
+    turn = run(turn, [leave_of(chunks[0])])
+    turn = project_some(turn, chunks[1:2])
+    turn = run(turn, [leave_of(chunks[1])])
+    turn = project_some(turn, chunks[2:4])
     for time in range(len(lanes[0]) + 6):
         for lane in lanes:
             turn = run(turn, jobs_of({time - i: c for i, c in enumerate(lane)}))
@@ -458,12 +464,10 @@
                 out, turn = place(
                     turn, c["theirs_sent"], c["theirs"], out, c["base"], (tokens, columns)
                 )
-        for lane in lanes:
-            if time < len(lane):
+            if 0 < time < len(lane):
                 turn = run(turn, [leave_of(lane[time])])
-        some = chunks[2 * time + 2 : 2 * time + 4]
-        if some:
-            turn = project_some(turn, some)
+                if time + 1 < len(lane):
+                    turn = project_some(turn, [lane[time + 1]])
     return out
 
 

time: 167 us -> 158 us (0.946)
  waiting for transfers between devices: 34.1 us -> 24 us
  Pallas kernels: 42.9 us -> 46.5 us
    ppermute x60, waiting for transfers between devices: 34.1 us -> 24 us  [swap(): return lax.ppermute(x, 'tensor', [(d, d ^ bits) for d in range(devices)])]
    pallas_call x39 -> x42, Pallas kernels: 40.5 us -> 44 us  [call(): pl.pallas_call(in_order(kernel, len(args), len(out_shapes)), out_shape=[*...]
  transfers between devices with their start and end apart: 68 -> 68, of which waited for: 19 -> 17; matrix products, arithmetic and copies ran while one was open for 0% -> 0% of each run, Pallas kernels for 17% -> 19%
where the time goes in v3:
time: 158 us
  starting transfers between devices  84.7 us (54%)
  Pallas kernels  46.5 us (29%)
  waiting for transfers between devices  24 us (15%)
  between operations  2.04 us (1%)
    ppermute x60, starting transfers between devices, swap(): return lax.ppermute(x, 'tensor', [(d, d ^ bits) for d in range(devices)])  79.4 us
    pallas_call x42, Pallas kernels, call(): pl.pallas_call(in_order(kernel, len(args), len(out_shapes)), out_shape=[*...  44 us
    ppermute x60, waiting for transfers between devices, swap(): return lax.ppermute(x, 'tensor', [(d, d ^ bits) for d in range(devices)])  24 us
    ppermute x8, starting transfers between devices, along(): return lax.ppermute(x, 'tensor', perm)  5.34 us
  transfers between devices with their start and end apart: 68, of which 17 were waited for; matrix products, arithmetic and copies ran while one was open for 0% of the time, Pallas kernels for 19%

profile of v3, /device:TPU:1, one launch (start us, length us, event | category | flops | bytes accessed | tf_op | source)
XLA Modules:
  0.0 158.1 jit_solution(6413007422118582346)
XLA Ops:
  0.7 2.5 %pack_kv.1 = (bf16[256,1024]{1,0:T(8,128)(2,1)}, bf16[272,128]{1,0:T(8,128)(2,1)}, bf16[272,128]{1,0:T(8,128)(2,1)}, bf16[272,128]{1,0:T(8,128)(2,1)}, bf16[272,...) custom-call(s32[1]{0:T(128)S(6)} %copy.21.lengths_ref, ...), custom_call_target="tpu_custom_call" | custom-call | tf_op jit(solution)/shard_map/pack_kv/pallas_call | solution.py:58
  3.2 5.2 %collective-permute-start = (bf16[272,128]{1,0:T(8,128)(2,1)}, bf16[272,128]{1,0:T(8,128)(2,1)S(1)}, u32[]{:S(2)}, u32[]{:S(2)}) collective-permute-start(bf16[272,128]{1,0:T(8,128)(2,1)} %get-tuple-element.145), channel_id=1, source_target_pairs={{0,14},{1,15},{2,12},{3,13},{4,10},{5,11},{6,8},{7,9},{8,6},{9,7},... | collective-permute-start | bytes 208904 | tf_op jit(solution)/shard_map/ppermute | solution.py:383
  13.8 4.5 %collective-permute-done.2.refs_2_ = bf16[272,128]{1,0:T(8,128)(2,1)S(1)} collective-permute-done((bf16[272,128]{1,0:T(8,128)(2,1)}, bf16[272,128]{1,0:T(8,128)(2,1)S(1)}, u32[]{:S(2)}, u32[]{:S(2)}) %collective-permute-start.2) | collective-permute-done | bytes 69664 | tf_op jit(solution)/shard_map/ppermute | solution.py:383
  23.1 4.1 %attention_mine.1 = (f32[256,1024]{1,0:T(8,128)S(1)}, f32[256,8]{1,0:T(8,128)S(1)}, f32[256,8]{1,0:T(8,128)S(1)}, f32[8,128]{1,0:T(8,128)S(1)}) custom-call(s32[1]{0:T(128)S(6)} %copy.22.refs_0_, bf16[256,1024]{1,0:T(8,128)(2,1)S(1)} %copy-done, bf16[8,272,128]{2,1,0:T(8,128)(2,1)S(1)} %get-tuple-element.153.refs_2_, f32[8,128]{1,0:T(8,128)S(1)} %get-tuple-element.154.refs_3_), custom_call_target="tpu_custom_call" | custom-call | flops 3000000000 | bytes 16777216 | tf_op jit(solution)/shard_map/attention_mine/pallas_call | solution.py:194
  27.2 5.4 %attention_theirs.1 = (bf16[256,1024]{1,0:T(8,128)(2,1)S(1)}, f32[8,128]{1,0:T(8,128)S(1)}) custom-call(s32[1]{0:T(128)S(6)} %copy.22.refs_0_, bf16[256,1024]{1,0:T(8,128)(2,1)S(1)} %copy-done, bf16[8,272,128]{2,1,0:T(8,128)(2,1)S(1)} %collective-permute-done.7.refs_2_, f32[256,1024]{1,0:T(8,128)S(1)} %get-tuple-element.155.refs_3_, ...), custom_call_target="tpu_custom_call" | custom-call | flops 3000000000 | bytes 16777216 | tf_op jit(solution)/shard_map/attention_theirs/pallas_call | solution.py:194
  32.6 3.0 %project.7 = (bf16[128,1024]{1,0:T(8,128)(2,1)S(1)}, bf16[128,1024]{1,0:T(8,128)(2,1)S(1)}, bf16[128,1024]{1,0:T(8,128)(2,1)S(1)}, bf16[128,1024]{1,0:T(8,128)(2,1)S(1)}, f32[8,128]{1,0:T(8,128)S(1)}) custom-call(bf16[256,1024]{1,0:T(8,128)(2,1)S(1)} %get-tuple-element.159.refs_0_, bf16[1024,16384]{1,0:T(8,128)(2,1)} %refs_1_.13, ...), custom_call_target="tpu_custom_call" | custom-call | flops 3000000000 | bytes 131072 | tf_op jit(solution)/shard_map/project/pallas_call | solution.py:194
  37.3 3.0 %project.8 = (bf16[128,1024]{1,0:T(8,128)(2,1)S(1)}, bf16[128,1024]{1,0:T(8,128)(2,1)S(1)}, bf16[128,1024]{1,0:T(8,128)(2,1)S(1)}, bf16[128,1024]{1,0:T(8,128)(2,1)S(1)}, f32[8,128]{1,0:T(8,128)S(1)}) custom-call(bf16[256,1024]{1,0:T(8,128)(2,1)S(1)} %get-tuple-element.159.refs_0_, bf16[1024,16384]{1,0:T(8,128)(2,1)} %refs_1_.13, ...), custom_call_target="tpu_custom_call" | custom-call | flops 3000000000 | bytes 131072 | tf_op jit(solution)/shard_map/project/pallas_call | solution.py:194
  42.0 4.7 %project.9 = (bf16[128,1024]{1,0:T(8,128)(2,1)S(1)}, bf16[128,1024]{1,0:T(8,128)(2,1)S(1)}, bf16[128,1024]{1,0:T(8,128)(2,1)S(1)}, bf16[128,1024]{1,0:T(8,128)(2...) custom-call(bf16[256,1024]{1,0:T(8,128)(2,1)S(1)} %get-tuple-element, ...), custom_call_target="tpu_custom_call" | custom-call | flops 3000000000 | bytes 131072 | tf_op jit(solution)/shard_map/project/pallas_call | solution.py:194
  52.4 3.0 %project.10 = (bf16[128,1024]{1,0:T(8,128)(2,1)S(1)}, bf16[128,1024]{1,0:T(8,128)(2,1)S(1)}, bf16[128,1024]{1,0:T(8,128)(2,1)S(1)}, bf16[128,1024]{1,0:T(8,128)(2,1)S(1)}, f32[8,128]{1,0:T(8,128)S(1)}) custom-call(bf16[256,1024]{1,0:T(8,128)(2,1)S(1)} %get-tuple-element.159.refs_0_, bf16[1024,16384]{1,0:T(8,128)(2,1)} %refs_1_.13, ...), custom_call_target="tpu_custom_call" | custom-call | flops 3000000000 | bytes 131072 | tf_op jit(solution)/shard_map/project/pallas_call | solution.py:194
  57.0 3.0 %project.11 = (bf16[128,1024]{1,0:T(8,128)(2,1)S(1)}, bf16[128,1024]{1,0:T(8,128)(2,1)S(1)}, bf16[128,1024]{1,0:T(8,128)(2,1)S(1)}, bf16[128,1024]{1,0:T(8,128)(2,1)S(1)}, f32[8,128]{1,0:T(8,128)S(1)}) custom-call(bf16[256,1024]{1,0:T(8,128)(2,1)S(1)} %get-tuple-element.159.refs_0_, bf16[1024,16384]{1,0:T(8,128)(2,1)} %refs_1_.13, ...), custom_call_target="tpu_custom_call" | custom-call | flops 3000000000 | bytes 131072 | tf_op jit(solution)/shard_map/project/pallas_call | solution.py:194
  65.6 3.0 %project.12 = (bf16[128,1024]{1,0:T(8,128)(2,1)S(1)}, bf16[128,1024]{1,0:T(8,128)(2,1)S(1)}, bf16[128,1024]{1,0:T(8,128)(2,1)S(1)}, bf16[128,1024]{1,0:T(8,128)(2,1)S(1)}, f32[8,128]{1,0:T(8,128)S(1)}) custom-call(bf16[256,1024]{1,0:T(8,128)(2,1)S(1)} %get-tuple-element.159.refs_0_, bf16[1024,16384]{1,0:T(8,128)(2,1)} %refs_1_.13, ...), custom_call_target="tpu_custom_call" | custom-call | flops 3000000000 | bytes 131072 | tf_op jit(solution)/shard_map/project/pallas_call | solution.py:194
  70.4 4.4 %collective-permute-start.32 = (bf16[128,1024]{1,0:T(8,128)(2,1)S(1)}, bf16[128,1024]{1,0:T(8,128)(2,1)S(1)}, u32[]{:S(2)}, u32[]{:S(2)}) collective-permute-start(bf16[128,1024]{1,0:T(8,128)(2,1)S(1)} %get-tuple-element.213), channel_id=1, source_target_pairs={{0,4},{1,5},{2,6},{3,7},{4,0},{5,1},{6,2},{7,3},{8,12},{9,13},{10,... | collective-permute-start | bytes 786440 | tf_op jit(solution)/shard_map/ppermute | solution.py:383
  74.9 3.0 %project.13 = (bf16[128,1024]{1,0:T(8,128)(2,1)S(1)}, bf16[128,1024]{1,0:T(8,128)(2,1)S(1)}, bf16[128,1024]{1,0:T(8,128)(2,1)S(1)}, bf16[128,1024]{1,0:T(8,128)(2,1)S(1)}, f32[8,128]{1,0:T(8,128)S(1)}) custom-call(bf16[256,1024]{1,0:T(8,128)(2,1)S(1)} %get-tuple-element.159.refs_0_, bf16[1024,16384]{1,0:T(8,128)(2,1)} %refs_1_.13, ...), custom_call_target="tpu_custom_call" | custom-call | flops 3000000000 | bytes 131072 | tf_op jit(solution)/shard_map/project/pallas_call | solution.py:194
  83.5 2.6 %collective-permute-start.35 = (bf16[128,1024]{1,0:T(8,128)(2,1)S(1)}, bf16[128,1024]{1,0:T(8,128)(2,1)S(1)}, u32[]{:S(2)}, u32[]{:S(2)}) collective-permute-start(bf16[128,1024]{1,0:T(8,128)(2,1)S(1)} %get-tuple-element.222), channel_id=1, source_target_pairs={{0,1},{1,0},{2,3},{3,2},{4,5},{5,4},{6,7},{7,6},{8,9},{9,8},{10,11... | collective-permute-start | bytes 786440 | tf_op jit(solution)/shard_map/ppermute | solution.py:383
  90.9 5.4 %collective-permute-done.40.refs_4_.refs_6_ = bf16[128,1024]{1,0:T(8,128)(2,1)S(1)} collective-permute-done((bf16[128,1024]{1,0:T(8,128)(2,1)S(1)}, bf16[128,1024]{1,0:T(8,128)(2,1)S(1)}, u32[]{:S(2)}, u32[]{:S(2)}) %collective-permute-start.40) | collective-permute-done | bytes 262176 | tf_op jit(solution)/shard_map/ppermute | solution.py:383
  97.3 2.7 %collective-permute-start.45 = (bf16[128,1024]{1,0:T(8,128)(2,1)S(1)}, bf16[128,1024]{1,0:T(8,128)(2,1)S(1)}, u32[]{:S(2)}, u32[]{:S(2)}) collective-permute-start(bf16[128,1024]{1,0:T(8,128)(2,1)S(1)} %get-tuple-element.236.refs_1_), channel_id=1, source_target_pairs={{0,4},{1,5},{2,6},{3,7},{4,0},{5,1},{6,2},{7,3},{8,12},{9,13},{10,... | collective-permute-start | bytes 786440 | tf_op jit(solution)/shard_map/ppermute | solution.py:383
  103.2 3.1 %collective-permute-start.42 = (bf16[128,1024]{1,0:T(8,128)(2,1)S(1)}, bf16[128,1024]{1,0:T(8,128)(2,1)S(1)}, u32[]{:S(2)}, u32[]{:S(2)}) collective-permute-start(bf16[128,1024]{1,0:T(8,128)(2,1)S(1)} %get-tuple-element.233.refs_1_), channel_id=1, source_target_pairs={{0,4},{1,5},{2,6},{3,7},{4,0},{5,1},{6,2},{7,3},{8,12},{9,13},{10,... | collective-permute-start | bytes 786440 | tf_op jit(solution)/shard_map/ppermute | solution.py:383
  109.6 2.4 %collective-permute-start.52 = (bf16[128,1024]{1,0:T(8,128)(2,1)S(1)}, bf16[128,1024]{1,0:T(8,128)(2,1)S(1)}, u32[]{:S(2)}, u32[]{:S(2)}) collective-permute-start(bf16[128,1024]{1,0:T(8,128)(2,1)S(1)} %get-tuple-element.245.refs_1_), channel_id=1, source_target_pairs={{0,4},{1,5},{2,6},{3,7},{4,0},{5,1},{6,2},{7,3},{8,12},{9,13},{10,... | collective-permute-start | bytes 786440 | tf_op jit(solution)/shard_map/ppermute | solution.py:383
  114.8 4.5 %collective-permute-start.51 = (bf16[2,128,1024]{2,1,0:T(8,128)(2,1)S(1)}, bf16[2,128,1024]{2,1,0:T(8,128)(2,1)S(1)}, u32[]{:S(2)}, u32[]{:S(2)}) collective-permute-start(bf16[2,128,1024]{2,1,0:T(8,128)(2,1)S(1)} %get-tuple-element.244.refs_0_), channel_id=1, source_target_pairs={{0,1},{1,0},{2,3},{3,2},{4,5},{5,4},{6,7},{7,6},{8,9},{9,8},{10,11... | collective-permute-start | bytes 1572872 | tf_op jit(solution)/shard_map/ppermute | solution.py:383
  119.5 2.7 %collective-permute-start.48 = (bf16[128,1024]{1,0:T(8,128)(2,1)S(1)}, bf16[128,1024]{1,0:T(8,128)(2,1)S(1)}, u32[]{:S(2)}, u32[]{:S(2)}) collective-permute-start(bf16[128,1024]{1,0:T(8,128)(2,1)S(1)} %get-tuple-element.241.refs_1_), channel_id=1, source_target_pairs={{0,4},{1,5},{2,6},{3,7},{4,0},{5,1},{6,2},{7,3},{8,12},{9,13},{10,... | collective-permute-start | bytes 786440 | tf_op jit(solution)/shard_map/ppermute | solution.py:383
  124.7 2.3 %collective-permute-start.59 = (bf16[128,1024]{1,0:T(8,128)(2,1)S(1)}, bf16[128,1024]{1,0:T(8,128)(2,1)S(1)}, u32[]{:S(2)}, u32[]{:S(2)}) collective-permute-start(bf16[128,1024]{1,0:T(8,128)(2,1)S(1)} %get-tuple-element.258.refs_1_), channel_id=1, source_target_pairs={{0,4},{1,5},{2,6},{3,7},{4,0},{5,1},{6,2},{7,3},{8,12},{9,13},{10,... | collective-permute-start | bytes 786440 | tf_op jit(solution)/shard_map/ppermute | solution.py:383
  136.3 3.4 %collective-permute-start.62 = (bf16[2,128,1024]{2,1,0:T(8,128)(2,1)S(1)}, bf16[2,128,1024]{2,1,0:T(8,128)(2,1)S(1)}, u32[]{:S(2)}, u32[]{:S(2)}) collective-permute-start(bf16[2,128,1024]{2,1,0:T(8,128)(2,1)S(1)} %get-tuple-element.264.refs_0_), channel_id=1, source_target_pairs={{0,1},{1,0},{2,3},{3,2},{4,5},{5,4},{6,7},{7,6},{8,9},{9,8},{10,11... | collective-permute-start | bytes 1572872 | tf_op jit(solution)/shard_map/ppermute | solution.py:383
  142.2 3.1 %collective-permute-start.67 = (bf16[2,128,1024]{2,1,0:T(8,128)(2,1)S(1)}, bf16[2,128,1024]{2,1,0:T(8,128)(2,1)S(1)}, u32[]{:S(2)}, u32[]{:S(2)}) collective-permute-start(bf16[2,128,1024]{2,1,0:T(8,128)(2,1)S(1)} %get-tuple-element.275.refs_0_), channel_id=1, source_target_pairs={{0,1},{1,0},{2,3},{3,2},{4,5},{5,4},{6,7},{7,6},{8,9},{9,8},{10,11... | collective-permute-start | bytes 1572872 | tf_op jit(solution)/shard_map/ppermute | solution.py:383
  147.0 2.8 %collective-permute-start.66 = (bf16[2,128,1024]{2,1,0:T(8,128)(2,1)S(1)}, bf16[2,128,1024]{2,1,0:T(8,128)(2,1)S(1)}, u32[]{:S(2)}, u32[]{:S(2)}) collective-permute-start(bf16[2,128,1024]{2,1,0:T(8,128)(2,1)S(1)} %get-tuple-element.274.refs_0_), channel_id=1, source_target_pairs={{0,1},{1,0},{2,3},{3,2},{4,5},{5,4},{6,7},{7,6},{8,9},{9,8},{10,11... | collective-permute-start | bytes 1572872 | tf_op jit(solution)/shard_map/ppermute | solution.py:383
  (160 shorter events, 72.1 us)
Async XLA Ops:
  8.3 10.0 %collective-permute-start.2 = (bf16[272,128]{1,0:T(8,128)(2,1)}, bf16[272,128]{1,0:T(8,128)(2,1)S(1)}, u32[]{:S(2)}, u32[]{:S(2)}) collective-permute-start(bf16[272,128]{1,0:T(8,128)(2,1)} %get-tuple-element.147), channel_id=1, source_target_pairs={{0,10},{1,11},{2,8},{3,9},{4,14},{5,15},{6,12},{7,13},{8,2},{9,3},... | collective-permute-start | bytes 208904 | tf_op jit(solution)/shard_map/ppermute | solution.py:383
  8.7 11.5 %collective-permute-start.3 = (bf16[272,128]{1,0:T(8,128)(2,1)}, bf16[272,128]{1,0:T(8,128)(2,1)S(1)}, u32[]{:S(2)}, u32[]{:S(2)}) collective-permute-start(bf16[272,128]{1,0:T(8,128)(2,1)} %get-tuple-element.148), channel_id=1, source_target_pairs={{0,8},{1,9},{2,10},{3,11},{4,12},{5,13},{6,14},{7,15},{8,0},{9,1},... | collective-permute-start | bytes 208904 | tf_op jit(solution)/shard_map/ppermute | solution.py:383
  41.4 14.1 %collective-permute-start.11 = (bf16[128,1024]{1,0:T(8,128)(2,1)S(1)}, bf16[128,1024]{1,0:T(8,128)(2,1)S(1)}, u32[]{:S(2)}, u32[]{:S(2)}) collective-permute-start(bf16[128,1024]{1,0:T(8,128)(2,1)S(1)} %get-tuple-element.172), channel_id=1, source_target_pairs={{0,1},{1,0},{2,3},{3,2},{4,5},{5,4},{6,7},{7,6},{8,9},{9,8},{10,11... | collective-permute-start | bytes 786440 | tf_op jit(solution)/shard_map/ppermute | solution.py:383
  48.8 11.3 %collective-permute-start.24 = (bf16[128,1024]{1,0:T(8,128)(2,1)S(1)}, bf16[128,1024]{1,0:T(8,128)(2,1)S(1)}, u32[]{:S(2)}, u32[]{:S(2)}) collective-permute-start(bf16[128,1024]{1,0:T(8,128)(2,1)S(1)} %get-tuple-element.198), channel_id=1, source_target_pairs={{0,4},{1,5},{2,6},{3,7},{4,0},{5,1},{6,2},{7,3},{8,12},{9,13},{10,... | collective-permute-start | bytes 786440 | tf_op jit(solution)/shard_map/ppermute | solution.py:383
  51.1 10.1 %collective-permute-start.22 = (bf16[128,1024]{1,0:T(8,128)(2,1)S(1)}, bf16[128,1024]{1,0:T(8,128)(2,1)S(1)}, u32[]{:S(2)}, u32[]{:S(2)}) collective-permute-start(bf16[128,1024]{1,0:T(8,128)(2,1)S(1)} %get-tuple-element.196), channel_id=1, source_target_pairs={{0,1},{1,0},{2,3},{3,2},{4,5},{5,4},{6,7},{7,6},{8,9},{9,8},{10,11... | collective-permute-start | bytes 786440 | tf_op jit(solution)/shard_map/ppermute | solution.py:383
  55.5 13.2 %collective-permute-start.18 = (bf16[128,1024]{1,0:T(8,128)(2,1)S(1)}, bf16[128,1024]{1,0:T(8,128)(2,1)S(1)}, u32[]{:S(2)}, u32[]{:S(2)}) collective-permute-start(bf16[128,1024]{1,0:T(8,128)(2,1)S(1)} %get-tuple-element.190), channel_id=1, source_target_pairs={{0,1},{1,0},{2,3},{3,2},{4,5},{5,4},{6,7},{7,6},{8,9},{9,8},{10,11... | collective-permute-start | bytes 786440 | tf_op jit(solution)/shard_map/ppermute | solution.py:383
  65.5 12.5 %collective-permute-start.29 = (bf16[128,1024]{1,0:T(8,128)(2,1)S(1)}, bf16[128,1024]{1,0:T(8,128)(2,1)S(1)}, u32[]{:S(2)}, u32[]{:S(2)}) collective-permute-start(bf16[128,1024]{1,0:T(8,128)(2,1)S(1)} %get-tuple-element.210), channel_id=1, source_target_pairs={{0,1},{1,0},{2,3},{3,2},{4,5},{5,4},{6,7},{7,6},{8,9},{9,8},{10,11... | collective-permute-start | bytes 786440 | tf_op jit(solution)/shard_map/ppermute | solution.py:383
  68.7 17.5 %collective-permute-start.16 = (bf16[128,1024]{1,0:T(8,128)(2,1)S(1)}, bf16[128,1024]{1,0:T(8,128)(2,1)S(1)}, u32[]{:S(2)}, u32[]{:S(2)}) collective-permute-start(bf16[128,1024]{1,0:T(8,128)(2,1)S(1)} %get-tuple-element.186), channel_id=1, source_target_pairs={{0,1},{1,0},{2,3},{3,2},{4,5},{5,4},{6,7},{7,6},{8,9},{9,8},{10,11... | collective-permute-start | bytes 786440 | tf_op jit(solution)/shard_map/ppermute | solution.py:383
  69.2 10.4 %collective-permute-start.30 = (bf16[128,1024]{1,0:T(8,128)(2,1)S(1)}, bf16[128,1024]{1,0:T(8,128)(2,1)S(1)}, u32[]{:S(2)}, u32[]{:S(2)}) collective-permute-start(bf16[128,1024]{1,0:T(8,128)(2,1)S(1)} %get-tuple-element.211), channel_id=1, source_target_pairs={{0,2},{1,3},{2,0},{3,1},{4,6},{5,7},{6,4},{7,5},{8,10},{9,11},{10,... | collective-permute-start | bytes 786440 | tf_op jit(solution)/shard_map/ppermute | solution.py:383
  69.5 11.0 %collective-permute-start.31 = (bf16[128,1024]{1,0:T(8,128)(2,1)S(1)}, bf16[128,1024]{1,0:T(8,128)(2,1)S(1)}, u32[]{:S(2)}, u32[]{:S(2)}) collective-permute-start(bf16[128,1024]{1,0:T(8,128)(2,1)S(1)} %get-tuple-element.212.refs_3_), channel_id=1, source_target_pairs={{4,8},{5,9},{6,10},{7,11},{8,4},{9,5},{10,6},{11,7},{20,24},{21,25... | collective-permute-start | bytes 786440 | tf_op jit(solution)/shard_map/ppermute | solution.py:387
  70.4 10.7 %collective-permute-start.32 = (bf16[128,1024]{1,0:T(8,128)(2,1)S(1)}, bf16[128,1024]{1,0:T(8,128)(2,1)S(1)}, u32[]{:S(2)}, u32[]{:S(2)}) collective-permute-start(bf16[128,1024]{1,0:T(8,128)(2,1)S(1)} %get-tuple-element.213), channel_id=1, source_target_pairs={{0,4},{1,5},{2,6},{3,7},{4,0},{5,1},{6,2},{7,3},{8,12},{9,13},{10,... | collective-permute-start | bytes 786440 | tf_op jit(solution)/shard_map/ppermute | solution.py:383
  87.5 12.5 %collective-permute-start.34 = (bf16[128,1024]{1,0:T(8,128)(2,1)S(1)}, bf16[128,1024]{1,0:T(8,128)(2,1)S(1)}, u32[]{:S(2)}, u32[]{:S(2)}) collective-permute-start(bf16[128,1024]{1,0:T(8,128)(2,1)S(1)} %get-tuple-element.220), channel_id=1, source_target_pairs={{0,1},{1,0},{2,3},{3,2},{4,5},{5,4},{6,7},{7,6},{8,9},{9,8},{10,11... | collective-permute-start | bytes 786440 | tf_op jit(solution)/shard_map/ppermute | solution.py:383
  90.2 11.8 %collective-permute-start.36 = (bf16[128,1024]{1,0:T(8,128)(2,1)S(1)}, bf16[128,1024]{1,0:T(8,128)(2,1)S(1)}, u32[]{:S(2)}, u32[]{:S(2)}) collective-permute-start(bf16[128,1024]{1,0:T(8,128)(2,1)S(1)} %get-tuple-element.224), channel_id=1, source_target_pairs={{0,2},{1,3},{2,0},{3,1},{4,6},{5,7},{6,4},{7,5},{8,10},{9,11},{10,... | collective-permute-start | bytes 786440 | tf_op jit(solution)/shard_map/ppermute | solution.py:383
  97.3 11.3 %collective-permute-start.45 = (bf16[128,1024]{1,0:T(8,128)(2,1)S(1)}, bf16[128,1024]{1,0:T(8,128)(2,1)S(1)}, u32[]{:S(2)}, u32[]{:S(2)}) collective-permute-start(bf16[128,1024]{1,0:T(8,128)(2,1)S(1)} %get-tuple-element.236.refs_1_), channel_id=1, source_target_pairs={{0,4},{1,5},{2,6},{3,7},{4,0},{5,1},{6,2},{7,3},{8,12},{9,13},{10,... | collective-permute-start | bytes 786440 | tf_op jit(solution)/shard_map/ppermute | solution.py:383
  103.2 10.8 %collective-permute-start.42 = (bf16[128,1024]{1,0:T(8,128)(2,1)S(1)}, bf16[128,1024]{1,0:T(8,128)(2,1)S(1)}, u32[]{:S(2)}, u32[]{:S(2)}) collective-permute-start(bf16[128,1024]{1,0:T(8,128)(2,1)S(1)} %get-tuple-element.233.refs_1_), channel_id=1, source_target_pairs={{0,4},{1,5},{2,6},{3,7},{4,0},{5,1},{6,2},{7,3},{8,12},{9,13},{10,... | collective-permute-start | bytes 786440 | tf_op jit(solution)/shard_map/ppermute | solution.py:383
  108.6 10.7 %collective-permute-start.44 = (bf16[128,1024]{1,0:T(8,128)(2,1)S(1)}, bf16[128,1024]{1,0:T(8,128)(2,1)S(1)}, u32[]{:S(2)}, u32[]{:S(2)}) collective-permute-start(bf16[128,1024]{1,0:T(8,128)(2,1)S(1)} %get-tuple-element.235.refs_8_), channel_id=1, source_target_pairs={{0,2},{1,3},{2,0},{3,1},{4,6},{5,7},{6,4},{7,5},{8,10},{9,11},{10,... | collective-permute-start | bytes 786440 | tf_op jit(solution)/shard_map/ppermute | solution.py:383
  109.6 12.6 %collective-permute-start.52 = (bf16[128,1024]{1,0:T(8,128)(2,1)S(1)}, bf16[128,1024]{1,0:T(8,128)(2,1)S(1)}, u32[]{:S(2)}, u32[]{:S(2)}) collective-permute-start(bf16[128,1024]{1,0:T(8,128)(2,1)S(1)} %get-tuple-element.245.refs_1_), channel_id=1, source_target_pairs={{0,4},{1,5},{2,6},{3,7},{4,0},{5,1},{6,2},{7,3},{8,12},{9,13},{10,... | collective-permute-start | bytes 786440 | tf_op jit(solution)/shard_map/ppermute | solution.py:383
  111.9 10.9 %collective-permute-start.53 = (bf16[128,1024]{1,0:T(8,128)(2,1)S(1)}, bf16[128,1024]{1,0:T(8,128)(2,1)S(1)}, u32[]{:S(2)}, u32[]{:S(2)}) collective-permute-start(bf16[128,1024]{1,0:T(8,128)(2,1)S(1)} %get-tuple-element.246.refs_2_), channel_id=1, source_target_pairs={{4,8},{5,9},{6,10},{7,11},{8,4},{9,5},{10,6},{11,7},{20,24},{21,25... | collective-permute-start | bytes 786440 | tf_op jit(solution)/shard_map/ppermute | solution.py:387
  124.7 10.1 %collective-permute-start.59 = (bf16[128,1024]{1,0:T(8,128)(2,1)S(1)}, bf16[128,1024]{1,0:T(8,128)(2,1)S(1)}, u32[]{:S(2)}, u32[]{:S(2)}) collective-permute-start(bf16[128,1024]{1,0:T(8,128)(2,1)S(1)} %get-tuple-element.258.refs_1_), channel_id=1, source_target_pairs={{0,4},{1,5},{2,6},{3,7},{4,0},{5,1},{6,2},{7,3},{8,12},{9,13},{10,... | collective-permute-start | bytes 786440 | tf_op jit(solution)/shard_map/ppermute | solution.py:383
  134.8 10.6 %collective-permute-start.63 = (bf16[2,128,1024]{2,1,0:T(8,128)(2,1)S(1)}, bf16[2,128,1024]{2,1,0:T(8,128)(2,1)S(1)}, u32[]{:S(2)}, u32[]{:S(2)}) collective-permute-start(bf16[2,128,1024]{2,1,0:T(8,128)(2,1)S(1)} %get-tuple-element.265.refs_0_), channel_id=1, source_target_pairs={{0,1},{1,0},{2,3},{3,2},{4,5},{5,4},{6,7},{7,6},{8,9},{9,8},{10,11... | collective-permute-start | bytes 1572872 | tf_op jit(solution)/shard_map/ppermute | solution.py:383
  135.5 11.5 %collective-permute-start.64 = (bf16[128,1024]{1,0:T(8,128)(2,1)S(1)}, bf16[128,1024]{1,0:T(8,128)(2,1)S(1)}, u32[]{:S(2)}, u32[]{:S(2)}) collective-permute-start(bf16[128,1024]{1,0:T(8,128)(2,1)S(1)} %get-tuple-element.269.refs_0_), channel_id=1, source_target_pairs={{0,2},{1,3},{2,0},{3,1},{4,6},{5,7},{6,4},{7,5},{8,10},{9,11},{10,... | collective-permute-start | bytes 786440 | tf_op jit(solution)/shard_map/ppermute | solution.py:383
  136.3 13.6 %collective-permute-start.62 = (bf16[2,128,1024]{2,1,0:T(8,128)(2,1)S(1)}, bf16[2,128,1024]{2,1,0:T(8,128)(2,1)S(1)}, u32[]{:S(2)}, u32[]{:S(2)}) collective-permute-start(bf16[2,128,1024]{2,1,0:T(8,128)(2,1)S(1)} %get-tuple-element.264.refs_0_), channel_id=1, source_target_pairs={{0,1},{1,0},{2,3},{3,2},{4,5},{5,4},{6,7},{7,6},{8,9},{9,8},{10,11... | collective-permute-start | bytes 1572872 | tf_op jit(solution)/shard_map/ppermute | solution.py:383
  141.4 11.2 %collective-permute-start.61 = (bf16[128,1024]{1,0:T(8,128)(2,1)S(1)}, bf16[128,1024]{1,0:T(8,128)(2,1)S(1)}, u32[]{:S(2)}, u32[]{:S(2)}) collective-permute-start(bf16[128,1024]{1,0:T(8,128)(2,1)S(1)} %get-tuple-element.263.refs_0_), channel_id=1, source_target_pairs={{0,2},{1,3},{2,0},{3,1},{4,6},{5,7},{6,4},{7,5},{8,10},{9,11},{10,... | collective-permute-start | bytes 786440 | tf_op jit(solution)/shard_map/ppermute | solution.py:383
  142.2 12.0 %collective-permute-start.67 = (bf16[2,128,1024]{2,1,0:T(8,128)(2,1)S(1)}, bf16[2,128,1024]{2,1,0:T(8,128)(2,1)S(1)}, u32[]{:S(2)}, u32[]{:S(2)}) collective-permute-start(bf16[2,128,1024]{2,1,0:T(8,128)(2,1)S(1)} %get-tuple-element.275.refs_0_), channel_id=1, source_target_pairs={{0,1},{1,0},{2,3},{3,2},{4,5},{5,4},{6,7},{7,6},{8,9},{9,8},{10,11... | collective-permute-start | bytes 1572872 | tf_op jit(solution)/shard_map/ppermute | solution.py:383
  (46 other events, 344.0 us)

commit v4 on v3

--- a/solution.py
+++ b/solution.py
@@ -419,10 +419,18 @@
 
     def jobs_of(at):
         jobs = []
+        if 5 in at:
+            c = at[5]
+            job = stack, [c["beside_sent"], c["beside"]], (2, *shape)
+            jobs.append((job, [c], "theirs", lambda x: swap(x, 1)))
         if 4 in at:
             c = at[4]
             job = choose, [c["near"], c["near_sent"]], shape
             jobs.append((job, [c], "beside", lambda x: swap(x, 2)))
+        if 2 in at:
+            c = at[2]
+            job = inward, [c["own"][1], c["core"][1], c["beside"], c["near"]], shape
+            jobs.append((job, [c], "across", lambda x: along(x, [(1, 2), (2, 1)])))
         early, late = at.get(1), at.get(3)
         if early or late:
             ins = [early["own"][1], early["core"][1], early["beside"]] if early else []
@@ -430,14 +438,6 @@
             job = join_and_middle if early and late else join if early else middle
             owners = [c for c in (early, late) if c]
             jobs.append(((job, ins, shape), owners, "near", lambda x: swap(x, 4)))
-        if 2 in at:
-            c = at[2]
-            job = inward, [c["own"][1], c["core"][1], c["beside"], c["near"]], shape
-            jobs.append((job, [c], "across", lambda x: along(x, [(1, 2), (2, 1)])))
-        if 5 in at:
-            c = at[5]
-            job = stack, [c["beside_sent"], c["beside"]], (2, *shape)
-            jobs.append((job, [c], "theirs", lambda x: swap(x, 1)))
         return jobs
 
     def run(turn, now):

time: 158 us -> 154 us (0.975)
  waiting for transfers between devices: 24 us -> 20.5 us
    ppermute x60, waiting for transfers between devices: 24 us -> 20.4 us  [swap(): return lax.ppermute(x, 'tensor', [(d, d ^ bits) for d in range(devices)])]
  transfers between devices with their start and end apart: 68 -> 68, of which waited for: 17 -> 17; matrix products, arithmetic and copies ran while one was open for 0% -> 0% of each run, Pallas kernels for 19% -> 20%
where the time goes in v4:
time: 154 us
  starting transfers between devices  83.7 us (54%)
  Pallas kernels  46.6 us (30%)
  waiting for transfers between devices  20.5 us (13%)
  between operations  2.06 us (1%)
    ppermute x60, starting transfers between devices, swap(): return lax.ppermute(x, 'tensor', [(d, d ^ bits) for d in range(devices)])  78.3 us
    pallas_call x42, Pallas kernels, call(): pl.pallas_call(in_order(kernel, len(args), len(out_shapes)), out_shape=[*...  44.1 us
    ppermute x60, waiting for transfers between devices, swap(): return lax.ppermute(x, 'tensor', [(d, d ^ bits) for d in range(devices)])  20.4 us
    ppermute x8, starting transfers between devices, along(): return lax.ppermute(x, 'tensor', perm)  5.35 us
  transfers between devices with their start and end apart: 68, of which 17 were waited for; matrix products, arithmetic and copies ran while one was open for 0% of the time, Pallas kernels for 20%

profile of v4, /device:TPU:1, one launch (start us, length us, event | category | flops | bytes accessed | tf_op | source)
XLA Modules:
  0.0 153.7 jit_solution(11929938457847041544)
XLA Ops:
  0.7 2.5 %pack_kv.1 = (bf16[256,1024]{1,0:T(8,128)(2,1)}, bf16[272,128]{1,0:T(8,128)(2,1)}, bf16[272,128]{1,0:T(8,128)(2,1)}, bf16[272,128]{1,0:T(8,128)(2,1)}, bf16[272,...) custom-call(s32[1]{0:T(128)S(6)} %copy.21.lengths_ref, ...), custom_call_target="tpu_custom_call" | custom-call | tf_op jit(solution)/shard_map/pack_kv/pallas_call | solution.py:58
  3.2 5.2 %collective-permute-start = (bf16[272,128]{1,0:T(8,128)(2,1)}, bf16[272,128]{1,0:T(8,128)(2,1)S(1)}, u32[]{:S(2)}, u32[]{:S(2)}) collective-permute-start(bf16[272,128]{1,0:T(8,128)(2,1)} %get-tuple-element.145), channel_id=1, source_target_pairs={{0,14},{1,15},{2,12},{3,13},{4,10},{5,11},{6,8},{7,9},{8,6},{9,7},... | collective-permute-start | bytes 208904 | tf_op jit(solution)/shard_map/ppermute | solution.py:383
  13.8 4.5 %collective-permute-done.2.refs_2_ = bf16[272,128]{1,0:T(8,128)(2,1)S(1)} collective-permute-done((bf16[272,128]{1,0:T(8,128)(2,1)}, bf16[272,128]{1,0:T(8,128)(2,1)S(1)}, u32[]{:S(2)}, u32[]{:S(2)}) %collective-permute-start.2) | collective-permute-done | bytes 69664 | tf_op jit(solution)/shard_map/ppermute | solution.py:383
  23.1 4.1 %attention_mine.1 = (f32[256,1024]{1,0:T(8,128)S(1)}, f32[256,8]{1,0:T(8,128)S(1)}, f32[256,8]{1,0:T(8,128)S(1)}, f32[8,128]{1,0:T(8,128)S(1)}) custom-call(s32[1]{0:T(128)S(6)} %copy.22.refs_0_, bf16[256,1024]{1,0:T(8,128)(2,1)S(1)} %copy-done, bf16[8,272,128]{2,1,0:T(8,128)(2,1)S(1)} %get-tuple-element.153.refs_2_, f32[8,128]{1,0:T(8,128)S(1)} %get-tuple-element.154.refs_3_), custom_call_target="tpu_custom_call" | custom-call | flops 3000000000 | bytes 16777216 | tf_op jit(solution)/shard_map/attention_mine/pallas_call | solution.py:194
  27.2 5.4 %attention_theirs.1 = (bf16[256,1024]{1,0:T(8,128)(2,1)S(1)}, f32[8,128]{1,0:T(8,128)S(1)}) custom-call(s32[1]{0:T(128)S(6)} %copy.22.refs_0_, bf16[256,1024]{1,0:T(8,128)(2,1)S(1)} %copy-done, bf16[8,272,128]{2,1,0:T(8,128)(2,1)S(1)} %collective-permute-done.7.refs_2_, f32[256,1024]{1,0:T(8,128)S(1)} %get-tuple-element.155.refs_3_, ...), custom_call_target="tpu_custom_call" | custom-call | flops 3000000000 | bytes 16777216 | tf_op jit(solution)/shard_map/attention_theirs/pallas_call | solution.py:194
  32.6 3.0 %project.7 = (bf16[128,1024]{1,0:T(8,128)(2,1)S(1)}, bf16[128,1024]{1,0:T(8,128)(2,1)S(1)}, bf16[128,1024]{1,0:T(8,128)(2,1)S(1)}, bf16[128,1024]{1,0:T(8,128)(2,1)S(1)}, f32[8,128]{1,0:T(8,128)S(1)}) custom-call(bf16[256,1024]{1,0:T(8,128)(2,1)S(1)} %get-tuple-element.159.refs_0_, bf16[1024,16384]{1,0:T(8,128)(2,1)} %refs_1_.13, ...), custom_call_target="tpu_custom_call" | custom-call | flops 3000000000 | bytes 131072 | tf_op jit(solution)/shard_map/project/pallas_call | solution.py:194
  37.3 3.0 %project.8 = (bf16[128,1024]{1,0:T(8,128)(2,1)S(1)}, bf16[128,1024]{1,0:T(8,128)(2,1)S(1)}, bf16[128,1024]{1,0:T(8,128)(2,1)S(1)}, bf16[128,1024]{1,0:T(8,128)(2,1)S(1)}, f32[8,128]{1,0:T(8,128)S(1)}) custom-call(bf16[256,1024]{1,0:T(8,128)(2,1)S(1)} %get-tuple-element.159.refs_0_, bf16[1024,16384]{1,0:T(8,128)(2,1)} %refs_1_.13, ...), custom_call_target="tpu_custom_call" | custom-call | flops 3000000000 | bytes 131072 | tf_op jit(solution)/shard_map/project/pallas_call | solution.py:194
  42.0 4.7 %project.9 = (bf16[128,1024]{1,0:T(8,128)(2,1)S(1)}, bf16[128,1024]{1,0:T(8,128)(2,1)S(1)}, bf16[128,1024]{1,0:T(8,128)(2,1)S(1)}, bf16[128,1024]{1,0:T(8,128)(2...) custom-call(bf16[256,1024]{1,0:T(8,128)(2,1)S(1)} %get-tuple-element, ...), custom_call_target="tpu_custom_call" | custom-call | flops 3000000000 | bytes 131072 | tf_op jit(solution)/shard_map/project/pallas_call | solution.py:194
  48.8 2.3 %collective-permute-start.20 = (bf16[128,1024]{1,0:T(8,128)(2,1)S(1)}, bf16[128,1024]{1,0:T(8,128)(2,1)S(1)}, u32[]{:S(2)}, u32[]{:S(2)}) collective-permute-start(bf16[128,1024]{1,0:T(8,128)(2,1)S(1)} %get-tuple-element.190), channel_id=1, source_target_pairs={{0,4},{1,5},{2,6},{3,7},{4,0},{5,1},{6,2},{7,3},{8,12},{9,13},{10,... | collective-permute-start | bytes 786440 | tf_op jit(solution)/shard_map/ppermute | solution.py:383
  52.4 3.0 %project.10 = (bf16[128,1024]{1,0:T(8,128)(2,1)S(1)}, bf16[128,1024]{1,0:T(8,128)(2,1)S(1)}, bf16[128,1024]{1,0:T(8,128)(2,1)S(1)}, bf16[128,1024]{1,0:T(8,128)(2,1)S(1)}, f32[8,128]{1,0:T(8,128)S(1)}) custom-call(bf16[256,1024]{1,0:T(8,128)(2,1)S(1)} %get-tuple-element.159.refs_0_, bf16[1024,16384]{1,0:T(8,128)(2,1)} %refs_1_.13, ...), custom_call_target="tpu_custom_call" | custom-call | flops 3000000000 | bytes 131072 | tf_op jit(solution)/shard_map/project/pallas_call | solution.py:194
  57.0 3.0 %project.11 = (bf16[128,1024]{1,0:T(8,128)(2,1)S(1)}, bf16[128,1024]{1,0:T(8,128)(2,1)S(1)}, bf16[128,1024]{1,0:T(8,128)(2,1)S(1)}, bf16[128,1024]{1,0:T(8,128)(2,1)S(1)}, f32[8,128]{1,0:T(8,128)S(1)}) custom-call(bf16[256,1024]{1,0:T(8,128)(2,1)S(1)} %get-tuple-element.159.refs_0_, bf16[1024,16384]{1,0:T(8,128)(2,1)} %refs_1_.13, ...), custom_call_target="tpu_custom_call" | custom-call | flops 3000000000 | bytes 131072 | tf_op jit(solution)/shard_map/project/pallas_call | solution.py:194
  63.1 2.1 %collective-permute-start.25 = (bf16[128,1024]{1,0:T(8,128)(2,1)S(1)}, bf16[128,1024]{1,0:T(8,128)(2,1)S(1)}, u32[]{:S(2)}, u32[]{:S(2)}) collective-permute-start(bf16[128,1024]{1,0:T(8,128)(2,1)S(1)} %get-tuple-element.203), channel_id=1, source_target_pairs={{0,1},{1,0},{2,3},{3,2},{4,5},{5,4},{6,7},{7,6},{8,9},{9,8},{10,11... | collective-permute-start | bytes 786440 | tf_op jit(solution)/shard_map/ppermute | solution.py:383
  65.6 3.0 %project.12 = (bf16[128,1024]{1,0:T(8,128)(2,1)S(1)}, bf16[128,1024]{1,0:T(8,128)(2,1)S(1)}, bf16[128,1024]{1,0:T(8,128)(2,1)S(1)}, bf16[128,1024]{1,0:T(8,128)(2,1)S(1)}, f32[8,128]{1,0:T(8,128)S(1)}) custom-call(bf16[256,1024]{1,0:T(8,128)(2,1)S(1)} %get-tuple-element.159.refs_0_, bf16[1024,16384]{1,0:T(8,128)(2,1)} %refs_1_.13, ...), custom_call_target="tpu_custom_call" | custom-call | flops 3000000000 | bytes 131072 | tf_op jit(solution)/shard_map/project/pallas_call | solution.py:194
  72.0 3.0 %project.13 = (bf16[128,1024]{1,0:T(8,128)(2,1)S(1)}, bf16[128,1024]{1,0:T(8,128)(2,1)S(1)}, bf16[128,1024]{1,0:T(8,128)(2,1)S(1)}, bf16[128,1024]{1,0:T(8,128)(2,1)S(1)}, f32[8,128]{1,0:T(8,128)S(1)}) custom-call(bf16[256,1024]{1,0:T(8,128)(2,1)S(1)} %get-tuple-element.159.refs_0_, bf16[1024,16384]{1,0:T(8,128)(2,1)} %refs_1_.13, ...), custom_call_target="tpu_custom_call" | custom-call | flops 3000000000 | bytes 131072 | tf_op jit(solution)/shard_map/project/pallas_call | solution.py:194
  77.3 3.7 %collective-permute-start.23 = (bf16[128,1024]{1,0:T(8,128)(2,1)S(1)}, bf16[128,1024]{1,0:T(8,128)(2,1)S(1)}, u32[]{:S(2)}, u32[]{:S(2)}) collective-permute-start(bf16[128,1024]{1,0:T(8,128)(2,1)S(1)} %get-tuple-element.199), channel_id=1, source_target_pairs={{0,4},{1,5},{2,6},{3,7},{4,0},{5,1},{6,2},{7,3},{8,12},{9,13},{10,... | collective-permute-start | bytes 786440 | tf_op jit(solution)/shard_map/ppermute | solution.py:383
  82.8 2.4 %collective-permute-start.34 = (bf16[128,1024]{1,0:T(8,128)(2,1)S(1)}, bf16[128,1024]{1,0:T(8,128)(2,1)S(1)}, u32[]{:S(2)}, u32[]{:S(2)}) collective-permute-start(bf16[128,1024]{1,0:T(8,128)(2,1)S(1)} %get-tuple-element.220), channel_id=1, source_target_pairs={{0,1},{1,0},{2,3},{3,2},{4,5},{5,4},{6,7},{7,6},{8,9},{9,8},{10,11... | collective-permute-start | bytes 786440 | tf_op jit(solution)/shard_map/ppermute | solution.py:383
  85.2 2.1 %collective-permute-done.23.refs_3_ = bf16[128,1024]{1,0:T(8,128)(2,1)S(1)} collective-permute-done((bf16[128,1024]{1,0:T(8,128)(2,1)S(1)}, bf16[128,1024]{1,0:T(8,128)(2,1)S(1)}, u32[]{:S(2)}, u32[]{:S(2)}) %collective-permute-start.23) | collective-permute-done | bytes 262176 | tf_op jit(solution)/shard_map/ppermute | solution.py:383
  91.5 2.8 %collective-permute-done.40.refs_8_.refs_6_ = bf16[128,1024]{1,0:T(8,128)(2,1)S(1)} collective-permute-done((bf16[128,1024]{1,0:T(8,128)(2,1)S(1)}, bf16[128,1024]{1,0:T(8,128)(2,1)S(1)}, u32[]{:S(2)}, u32[]{:S(2)}) %collective-permute-start.40) | collective-permute-done | bytes 262176 | tf_op jit(solution)/shard_map/ppermute | solution.py:383
  101.7 2.8 %collective-permute-start.43 = (bf16[128,1024]{1,0:T(8,128)(2,1)S(1)}, bf16[128,1024]{1,0:T(8,128)(2,1)S(1)}, u32[]{:S(2)}, u32[]{:S(2)}) collective-permute-start(bf16[128,1024]{1,0:T(8,128)(2,1)S(1)} %get-tuple-element.234.refs_3_), channel_id=1, source_target_pairs={{0,4},{1,5},{2,6},{3,7},{4,0},{5,1},{6,2},{7,3},{8,12},{9,13},{10,... | collective-permute-start | bytes 786440 | tf_op jit(solution)/shard_map/ppermute | solution.py:383
  107.2 3.9 %collective-permute-start.53 = (bf16[128,1024]{1,0:T(8,128)(2,1)S(1)}, bf16[128,1024]{1,0:T(8,128)(2,1)S(1)}, u32[]{:S(2)}, u32[]{:S(2)}) collective-permute-start(bf16[128,1024]{1,0:T(8,128)(2,1)S(1)} %get-tuple-element.246.refs_3_), channel_id=1, source_target_pairs={{0,4},{1,5},{2,6},{3,7},{4,0},{5,1},{6,2},{7,3},{8,12},{9,13},{10,... | collective-permute-start | bytes 786440 | tf_op jit(solution)/shard_map/ppermute | solution.py:383
  111.8 5.1 %collective-permute-start.51 = (bf16[2,128,1024]{2,1,0:T(8,128)(2,1)S(1)}, bf16[2,128,1024]{2,1,0:T(8,128)(2,1)S(1)}, u32[]{:S(2)}, u32[]{:S(2)}) collective-permute-start(bf16[2,128,1024]{2,1,0:T(8,128)(2,1)S(1)} %get-tuple-element.244.refs_0_), channel_id=1, source_target_pairs={{0,1},{1,0},{2,3},{3,2},{4,5},{5,4},{6,7},{7,6},{8,9},{9,8},{10,11... | collective-permute-start | bytes 1572872 | tf_op jit(solution)/shard_map/ppermute | solution.py:383
  120.8 3.2 %collective-permute-start.58 = (bf16[2,128,1024]{2,1,0:T(8,128)(2,1)S(1)}, bf16[2,128,1024]{2,1,0:T(8,128)(2,1)S(1)}, u32[]{:S(2)}, u32[]{:S(2)}) collective-permute-start(bf16[2,128,1024]{2,1,0:T(8,128)(2,1)S(1)} %get-tuple-element.254.refs_0_), channel_id=1, source_target_pairs={{0,1},{1,0},{2,3},{3,2},{4,5},{5,4},{6,7},{7,6},{8,9},{9,8},{10,11... | collective-permute-start | bytes 1572872 | tf_op jit(solution)/shard_map/ppermute | solution.py:383
  134.7 2.4 %collective-permute-start.62 = (bf16[2,128,1024]{2,1,0:T(8,128)(2,1)S(1)}, bf16[2,128,1024]{2,1,0:T(8,128)(2,1)S(1)}, u32[]{:S(2)}, u32[]{:S(2)}) collective-permute-start(bf16[2,128,1024]{2,1,0:T(8,128)(2,1)S(1)} %get-tuple-element.264.refs_0_), channel_id=1, source_target_pairs={{0,1},{1,0},{2,3},{3,2},{4,5},{5,4},{6,7},{7,6},{8,9},{9,8},{10,11... | collective-permute-start | bytes 1572872 | tf_op jit(solution)/shard_map/ppermute | solution.py:383
  146.1 2.4 %collective-permute-done.61.refs_1_ = bf16[128,1024]{1,0:T(8,128)(2,1)S(1)} collective-permute-done((bf16[128,1024]{1,0:T(8,128)(2,1)S(1)}, bf16[128,1024]{1,0:T(8,128)(2,1)S(1)}, u32[]{:S(2)}, u32[]{:S(2)}) %collective-permute-start.61) | collective-permute-done | bytes 262176 | tf_op jit(solution)/shard_map/ppermute | solution.py:383
  (160 shorter events, 71.8 us)
Async XLA Ops:
  3.2 9.6 %collective-permute-start = (bf16[272,128]{1,0:T(8,128)(2,1)}, bf16[272,128]{1,0:T(8,128)(2,1)S(1)}, u32[]{:S(2)}, u32[]{:S(2)}) collective-permute-start(bf16[272,128]{1,0:T(8,128)(2,1)} %get-tuple-element.145), channel_id=1, source_target_pairs={{0,14},{1,15},{2,12},{3,13},{4,10},{5,11},{6,8},{7,9},{8,6},{9,7},... | collective-permute-start | bytes 208904 | tf_op jit(solution)/shard_map/ppermute | solution.py:383
  8.3 10.0 %collective-permute-start.2 = (bf16[272,128]{1,0:T(8,128)(2,1)}, bf16[272,128]{1,0:T(8,128)(2,1)S(1)}, u32[]{:S(2)}, u32[]{:S(2)}) collective-permute-start(bf16[272,128]{1,0:T(8,128)(2,1)} %get-tuple-element.147), channel_id=1, source_target_pairs={{0,10},{1,11},{2,8},{3,9},{4,14},{5,15},{6,12},{7,13},{8,2},{9,3},... | collective-permute-start | bytes 208904 | tf_op jit(solution)/shard_map/ppermute | solution.py:383
  8.7 11.5 %collective-permute-start.3 = (bf16[272,128]{1,0:T(8,128)(2,1)}, bf16[272,128]{1,0:T(8,128)(2,1)S(1)}, u32[]{:S(2)}, u32[]{:S(2)}) collective-permute-start(bf16[272,128]{1,0:T(8,128)(2,1)} %get-tuple-element.148), channel_id=1, source_target_pairs={{0,8},{1,9},{2,10},{3,11},{4,12},{5,13},{6,14},{7,15},{8,0},{9,1},... | collective-permute-start | bytes 208904 | tf_op jit(solution)/shard_map/ppermute | solution.py:383
  10.8 9.5 %collective-permute-start.4 = (bf16[272,128]{1,0:T(8,128)(2,1)}, bf16[272,128]{1,0:T(8,128)(2,1)S(1)}, u32[]{:S(2)}, u32[]{:S(2)}) collective-permute-start(bf16[272,128]{1,0:T(8,128)(2,1)} %get-tuple-element.149), channel_id=1, source_target_pairs={{0,6},{1,7},{2,4},{3,5},{4,2},{5,3},{6,0},{7,1},{8,14},{9,15},{10,... | collective-permute-start | bytes 208904 | tf_op jit(solution)/shard_map/ppermute | solution.py:383
  41.4 14.1 %collective-permute-start.12 = (bf16[128,1024]{1,0:T(8,128)(2,1)S(1)}, bf16[128,1024]{1,0:T(8,128)(2,1)S(1)}, u32[]{:S(2)}, u32[]{:S(2)}) collective-permute-start(bf16[128,1024]{1,0:T(8,128)(2,1)S(1)} %get-tuple-element.174), channel_id=1, source_target_pairs={{0,1},{1,0},{2,3},{3,2},{4,5},{5,4},{6,7},{7,6},{8,9},{9,8},{10,11... | collective-permute-start | bytes 786440 | tf_op jit(solution)/shard_map/ppermute | solution.py:383
  48.8 11.3 %collective-permute-start.20 = (bf16[128,1024]{1,0:T(8,128)(2,1)S(1)}, bf16[128,1024]{1,0:T(8,128)(2,1)S(1)}, u32[]{:S(2)}, u32[]{:S(2)}) collective-permute-start(bf16[128,1024]{1,0:T(8,128)(2,1)S(1)} %get-tuple-element.190), channel_id=1, source_target_pairs={{0,4},{1,5},{2,6},{3,7},{4,0},{5,1},{6,2},{7,3},{8,12},{9,13},{10,... | collective-permute-start | bytes 786440 | tf_op jit(solution)/shard_map/ppermute | solution.py:383
  51.1 10.1 %collective-permute-start.21 = (bf16[128,1024]{1,0:T(8,128)(2,1)S(1)}, bf16[128,1024]{1,0:T(8,128)(2,1)S(1)}, u32[]{:S(2)}, u32[]{:S(2)}) collective-permute-start(bf16[128,1024]{1,0:T(8,128)(2,1)S(1)} %get-tuple-element.192), channel_id=1, source_target_pairs={{0,1},{1,0},{2,3},{3,2},{4,5},{5,4},{6,7},{7,6},{8,9},{9,8},{10,11... | collective-permute-start | bytes 786440 | tf_op jit(solution)/shard_map/ppermute | solution.py:383
  55.5 13.2 %collective-permute-start.10 = (bf16[128,1024]{1,0:T(8,128)(2,1)S(1)}, bf16[128,1024]{1,0:T(8,128)(2,1)S(1)}, u32[]{:S(2)}, u32[]{:S(2)}) collective-permute-start(bf16[128,1024]{1,0:T(8,128)(2,1)S(1)} %get-tuple-element.170), channel_id=1, source_target_pairs={{0,1},{1,0},{2,3},{3,2},{4,5},{5,4},{6,7},{7,6},{8,9},{9,8},{10,11... | collective-permute-start | bytes 786440 | tf_op jit(solution)/shard_map/ppermute | solution.py:383
  55.8 9.7 %collective-permute-start.19 = (bf16[128,1024]{1,0:T(8,128)(2,1)S(1)}, bf16[128,1024]{1,0:T(8,128)(2,1)S(1)}, u32[]{:S(2)}, u32[]{:S(2)}) collective-permute-start(bf16[128,1024]{1,0:T(8,128)(2,1)S(1)} %get-tuple-element.189), channel_id=1, source_target_pairs={{0,1},{1,0},{2,3},{3,2},{4,5},{5,4},{6,7},{7,6},{8,9},{9,8},{10,11... | collective-permute-start | bytes 786440 | tf_op jit(solution)/shard_map/ppermute | solution.py:383
  65.5 9.6 %collective-permute-start.30 = (bf16[128,1024]{1,0:T(8,128)(2,1)S(1)}, bf16[128,1024]{1,0:T(8,128)(2,1)S(1)}, u32[]{:S(2)}, u32[]{:S(2)}) collective-permute-start(bf16[128,1024]{1,0:T(8,128)(2,1)S(1)} %get-tuple-element.211), channel_id=1, source_target_pairs={{0,1},{1,0},{2,3},{3,2},{4,5},{5,4},{6,7},{7,6},{8,9},{9,8},{10,11... | collective-permute-start | bytes 786440 | tf_op jit(solution)/shard_map/ppermute | solution.py:383
  68.7 14.0 %collective-permute-start.24 = (bf16[128,1024]{1,0:T(8,128)(2,1)S(1)}, bf16[128,1024]{1,0:T(8,128)(2,1)S(1)}, u32[]{:S(2)}, u32[]{:S(2)}) collective-permute-start(bf16[128,1024]{1,0:T(8,128)(2,1)S(1)} %get-tuple-element.201), channel_id=1, source_target_pairs={{0,1},{1,0},{2,3},{3,2},{4,5},{5,4},{6,7},{7,6},{8,9},{9,8},{10,11... | collective-permute-start | bytes 786440 | tf_op jit(solution)/shard_map/ppermute | solution.py:383
  71.3 9.7 %collective-permute-start.32 = (bf16[128,1024]{1,0:T(8,128)(2,1)S(1)}, bf16[128,1024]{1,0:T(8,128)(2,1)S(1)}, u32[]{:S(2)}, u32[]{:S(2)}) collective-permute-start(bf16[128,1024]{1,0:T(8,128)(2,1)S(1)} %get-tuple-element.213.refs_7_), channel_id=1, source_target_pairs={{4,8},{5,9},{6,10},{7,11},{8,4},{9,5},{10,6},{11,7},{20,24},{21,25... | collective-permute-start | bytes 786440 | tf_op jit(solution)/shard_map/ppermute | solution.py:387
  77.3 10.1 %collective-permute-start.23 = (bf16[128,1024]{1,0:T(8,128)(2,1)S(1)}, bf16[128,1024]{1,0:T(8,128)(2,1)S(1)}, u32[]{:S(2)}, u32[]{:S(2)}) collective-permute-start(bf16[128,1024]{1,0:T(8,128)(2,1)S(1)} %get-tuple-element.199), channel_id=1, source_target_pairs={{0,4},{1,5},{2,6},{3,7},{4,0},{5,1},{6,2},{7,3},{8,12},{9,13},{10,... | collective-permute-start | bytes 786440 | tf_op jit(solution)/shard_map/ppermute | solution.py:383
  82.8 14.9 %collective-permute-start.34 = (bf16[128,1024]{1,0:T(8,128)(2,1)S(1)}, bf16[128,1024]{1,0:T(8,128)(2,1)S(1)}, u32[]{:S(2)}, u32[]{:S(2)}) collective-permute-start(bf16[128,1024]{1,0:T(8,128)(2,1)S(1)} %get-tuple-element.220), channel_id=1, source_target_pairs={{0,1},{1,0},{2,3},{3,2},{4,5},{5,4},{6,7},{7,6},{8,9},{9,8},{10,11... | collective-permute-start | bytes 786440 | tf_op jit(solution)/shard_map/ppermute | solution.py:383
  100.9 10.3 %collective-permute-start.42 = (bf16[128,1024]{1,0:T(8,128)(2,1)S(1)}, bf16[128,1024]{1,0:T(8,128)(2,1)S(1)}, u32[]{:S(2)}, u32[]{:S(2)}) collective-permute-start(bf16[128,1024]{1,0:T(8,128)(2,1)S(1)} %get-tuple-element.233.refs_0_), channel_id=1, source_target_pairs={{0,2},{1,3},{2,0},{3,1},{4,6},{5,7},{6,4},{7,5},{8,10},{9,11},{10,... | collective-permute-start | bytes 786440 | tf_op jit(solution)/shard_map/ppermute | solution.py:383
  101.7 10.1 %collective-permute-start.43 = (bf16[128,1024]{1,0:T(8,128)(2,1)S(1)}, bf16[128,1024]{1,0:T(8,128)(2,1)S(1)}, u32[]{:S(2)}, u32[]{:S(2)}) collective-permute-start(bf16[128,1024]{1,0:T(8,128)(2,1)S(1)} %get-tuple-element.234.refs_3_), channel_id=1, source_target_pairs={{0,4},{1,5},{2,6},{3,7},{4,0},{5,1},{6,2},{7,3},{8,12},{9,13},{10,... | collective-permute-start | bytes 786440 | tf_op jit(solution)/shard_map/ppermute | solution.py:383
  104.8 12.2 %collective-permute-start.44 = (bf16[128,1024]{1,0:T(8,128)(2,1)S(1)}, bf16[128,1024]{1,0:T(8,128)(2,1)S(1)}, u32[]{:S(2)}, u32[]{:S(2)}) collective-permute-start(bf16[128,1024]{1,0:T(8,128)(2,1)S(1)} %get-tuple-element.235.refs_8_), channel_id=1, source_target_pairs={{4,8},{5,9},{6,10},{7,11},{8,4},{9,5},{10,6},{11,7},{20,24},{21,25... | collective-permute-start | bytes 786440 | tf_op jit(solution)/shard_map/ppermute | solution.py:387
  106.2 12.1 %collective-permute-start.52 = (bf16[128,1024]{1,0:T(8,128)(2,1)S(1)}, bf16[128,1024]{1,0:T(8,128)(2,1)S(1)}, u32[]{:S(2)}, u32[]{:S(2)}) collective-permute-start(bf16[128,1024]{1,0:T(8,128)(2,1)S(1)} %get-tuple-element.245.refs_0_), channel_id=1, source_target_pairs={{0,2},{1,3},{2,0},{3,1},{4,6},{5,7},{6,4},{7,5},{8,10},{9,11},{10,... | collective-permute-start | bytes 786440 | tf_op jit(solution)/shard_map/ppermute | solution.py:383
  107.2 12.9 %collective-permute-start.53 = (bf16[128,1024]{1,0:T(8,128)(2,1)S(1)}, bf16[128,1024]{1,0:T(8,128)(2,1)S(1)}, u32[]{:S(2)}, u32[]{:S(2)}) collective-permute-start(bf16[128,1024]{1,0:T(8,128)(2,1)S(1)} %get-tuple-element.246.refs_3_), channel_id=1, source_target_pairs={{0,4},{1,5},{2,6},{3,7},{4,0},{5,1},{6,2},{7,3},{8,12},{9,13},{10,... | collective-permute-start | bytes 786440 | tf_op jit(solution)/shard_map/ppermute | solution.py:383
  111.2 9.6 %collective-permute-start.54 = (bf16[128,1024]{1,0:T(8,128)(2,1)S(1)}, bf16[128,1024]{1,0:T(8,128)(2,1)S(1)}, u32[]{:S(2)}, u32[]{:S(2)}) collective-permute-start(bf16[128,1024]{1,0:T(8,128)(2,1)S(1)} %get-tuple-element.247.refs_4_), channel_id=1, source_target_pairs={{4,8},{5,9},{6,10},{7,11},{8,4},{9,5},{10,6},{11,7},{20,24},{21,25... | collective-permute-start | bytes 786440 | tf_op jit(solution)/shard_map/ppermute | solution.py:387
  111.8 12.3 %collective-permute-start.51 = (bf16[2,128,1024]{2,1,0:T(8,128)(2,1)S(1)}, bf16[2,128,1024]{2,1,0:T(8,128)(2,1)S(1)}, u32[]{:S(2)}, u32[]{:S(2)}) collective-permute-start(bf16[2,128,1024]{2,1,0:T(8,128)(2,1)S(1)} %get-tuple-element.244.refs_0_), channel_id=1, source_target_pairs={{0,1},{1,0},{2,3},{3,2},{4,5},{5,4},{6,7},{7,6},{8,9},{9,8},{10,11... | collective-permute-start | bytes 1572872 | tf_op jit(solution)/shard_map/ppermute | solution.py:383
  134.7 10.4 %collective-permute-start.62 = (bf16[2,128,1024]{2,1,0:T(8,128)(2,1)S(1)}, bf16[2,128,1024]{2,1,0:T(8,128)(2,1)S(1)}, u32[]{:S(2)}, u32[]{:S(2)}) collective-permute-start(bf16[2,128,1024]{2,1,0:T(8,128)(2,1)S(1)} %get-tuple-element.264.refs_0_), channel_id=1, source_target_pairs={{0,1},{1,0},{2,3},{3,2},{4,5},{5,4},{6,7},{7,6},{8,9},{9,8},{10,11... | collective-permute-start | bytes 1572872 | tf_op jit(solution)/shard_map/ppermute | solution.py:383
  138.8 9.7 %collective-permute-start.61 = (bf16[128,1024]{1,0:T(8,128)(2,1)S(1)}, bf16[128,1024]{1,0:T(8,128)(2,1)S(1)}, u32[]{:S(2)}, u32[]{:S(2)}) collective-permute-start(bf16[128,1024]{1,0:T(8,128)(2,1)S(1)} %get-tuple-element.263.refs_0_), channel_id=1, source_target_pairs={{0,2},{1,3},{2,0},{3,1},{4,6},{5,7},{6,4},{7,5},{8,10},{9,11},{10,... | collective-permute-start | bytes 786440 | tf_op jit(solution)/shard_map/ppermute | solution.py:383
  139.6 10.2 %collective-permute-start.67 = (bf16[2,128,1024]{2,1,0:T(8,128)(2,1)S(1)}, bf16[2,128,1024]{2,1,0:T(8,128)(2,1)S(1)}, u32[]{:S(2)}, u32[]{:S(2)}) collective-permute-start(bf16[2,128,1024]{2,1,0:T(8,128)(2,1)S(1)} %get-tuple-element.275.refs_0_), channel_id=1, source_target_pairs={{0,1},{1,0},{2,3},{3,2},{4,5},{5,4},{6,7},{7,6},{8,9},{9,8},{10,11... | collective-permute-start | bytes 1572872 | tf_op jit(solution)/shard_map/ppermute | solution.py:383
  (46 other events, 340.1 us)
